TPU v7x, 32 devices: a whole 2x2x4 slice. The times are simulated.
32 devices in a mesh: rec: 8 (over z, y), src: 4 (over x, core).
Axes of the slice: x: 2, y: 2, z: 4, core: 2. Of those that a mesh axis runs over, the one named last changes fastest.
Arguments:
- kernel: float32 [2, 2, 5120, 5120], P(None, None, 'rec', 'src'), may hold values from -0.0625 to 0.0625
- traces: float32 [4, 2560, 2, 2, 256], P('src', 'rec')
- acq_lists: int32 [4, 2560], P('src', 'rec'), may hold values from 0 to 1279, as said below
- counts: int32 [4, 8], P('src', 'rec'), may hold values from 1 to 320, as said below
Outputs:
- solution: float32 [5120, 2, 2, 256], P(('src', 'rec'))
- next_left: float32 [5120, 2, 2, 256], P(('rec', 'src'))
Inputs may be any that keep to these rules, and one draw needn't show every extreme that they name: `acq_lists`: an id a * 160 + k names row k of area a. Within each list the first counts[s, r] slots of the blocks name every id exactly once; other slots hold ids to be ignored. No block names more than 40 ids of one area, and every block that names an area names exactly 40 of its ids. `counts`: used slots of a block; in every list some block uses all 320.
All inputs are finite; a program needn't handle non-finite values.
Results may differ from a plain program's by a relative error of at most 0.00026.
Values sent between devices are 32-bit elements; how exact they have to be, the bound alone decides.
No kernel may reach another device: no remote copies, remote signals or barrier semaphores. Data moves between devices by JAX's collectives and lax.ppermute only.
A program may use at most 128 MiB of HBM per device.

v0:
```python
import functools
import jax
import jax.numpy as jnp
from jax import lax
from jax.experimental import pallas as pl
from jax.experimental.pallas import tpu as pltpu
from jax.sharding import Mesh, PartitionSpec as P

FREQS = 2
SOURCES = 256
ITERS = 2
LANES = 128
HEAD = 8
CHUNKS = 2 * SOURCES // LANES
REC = ("z", "y")
SRC = ("x", "c")
VMEM_BYTES = 42 * 2**20
SMALL_VMEM_BYTES = 12 * 2**20


def split(values):
    high = values.astype(jnp.bfloat16)
    return high, (values - high.astype(jnp.float32)).astype(jnp.bfloat16)


def dot_three(left, right, dims):
    def dot(a, b):
        return lax.dot_general(a, b, (dims, ((), ())), preferred_element_type=jnp.float32)

    return dot(left[0], right[0]) + (dot(left[0], right[1]) + dot(left[1], right[0]))


def dot_exact(chosen, values):
    total = None
    for _ in range(3):
        part = values.astype(jnp.bfloat16)
        values = values - part.astype(jnp.float32)
        term = lax.dot_general(
            chosen, part, (((0,), (0,)), ((), ())), preferred_element_type=jnp.float32
        )
        total = term if total is None else total + term
    return total


def other(axis):
    index = lax.axis_index(axis)
    return index + 1 - 2 * lax.rem(index, 2)


def product_kernel(adjoint, places, outs, k_ref, *refs):
    piece_refs = refs[: len(places)]
    out_refs = refs[len(places) : len(places) + len(outs)]
    head, sum_high, sum_low, real_high, real_low, imag_high, imag_low, total = refs[
        len(places) + len(outs) :
    ]
    step = pl.program_id(0)
    half = real_high.shape[1]

    @pl.when(step == 0)
    def _():
        sums = None
        for place, piece in zip(places, piece_refs):
            rows = (piece.shape[0] - HEAD) // CHUNKS
            at = 0 if place is None else pl.multiple_of(place() * rows, rows)
            here = pl.ds(at, rows)
            for chunk in range(CHUNKS // 2):
                lanes = slice(chunk * LANES, (chunk + 1) * LANES)
                start = HEAD + chunk * rows
                real = piece[start : start + rows, :]
                start += CHUNKS // 2 * rows
                imag = piece[start : start + rows, :]
                if adjoint:
                    imag = -imag
                sum_high[here, lanes], sum_low[here, lanes] = split(real + imag)
                real_high[here, lanes], real_low[here, lanes] = split(real)
                imag_high[here, lanes], imag_low[here, lanes] = split(imag)
            sums = piece[:HEAD, :] if sums is None else sums + piece[:HEAD, :]
        head[...] = sums

    dims = ((0,), (0,)) if adjoint else ((1,), (0,))
    k_real, k_imag = k_ref[0, 0], k_ref[1, 0]
    first = dot_three(split(k_real), (sum_high[...], sum_low[...]), dims)
    second = dot_three(split(k_imag - k_real), (real_high[...], real_low[...]), dims)
    third = dot_three(split(k_real + k_imag), (imag_high[...], imag_low[...]), dims)
    rows = first.shape[0]
    at = pl.multiple_of(step * rows, rows)
    total[pl.ds(at, rows), :half] = first - third
    total[pl.ds(at, rows), half:] = -(first + second) if adjoint else first + second

    @pl.when(step == pl.num_programs(0) - 1)
    def _():
        for out, out_ref in zip(outs, out_refs):
            for slot, place in enumerate(out):
                target = out_ref.at[slot] if len(out) > 1 else out_ref
                rows = (target.shape[0] - HEAD) // CHUNKS
                at = 0 if place is None else pl.multiple_of(place() * rows, rows)
                target[:HEAD, :] = head[...]
                for chunk in range(CHUNKS):
                    lanes = slice(chunk * LANES, (chunk + 1) * LANES)
                    start = HEAD + chunk * rows
                    target[start : start + rows, :] = total[pl.ds(at, rows), lanes]


def product(kernel, slab, adjoint, pieces, places, outs, out_rows):
    rows, columns = kernel.shape[2:]
    width = 2 * SOURCES
    if adjoint:
        tile = columns // 2 if columns % 256 == 0 and columns > 640 else columns
        steps, shape, given, made = columns // tile, (2, 1, rows, tile), rows, columns
        k_spec = pl.BlockSpec(shape, lambda i: (0, slab, 0, i))
    else:
        tile = rows // 2
        steps, shape, given, made = rows // tile, (2, 1, tile, columns), columns, rows
        k_spec = pl.BlockSpec(shape, lambda i: (0, slab, i, 0))
    shapes = [
        ((len(out),) if len(out) > 1 else ()) + (HEAD + CHUNKS * out_rows, LANES) for out in outs
    ]
    return pl.pallas_call(
        functools.partial(product_kernel, adjoint, places, outs),
        grid=(steps,),
        in_specs=[k_spec] + [pl.BlockSpec(p.shape, lambda i: (0, 0)) for p in pieces],
        out_specs=[pl.BlockSpec(s, lambda i, n=len(s): (0,) * n) for s in shapes],
        out_shape=[jax.ShapeDtypeStruct(s, jnp.float32) for s in shapes],
        scratch_shapes=[pltpu.VMEM((HEAD, LANES), jnp.float32)]
        + [pltpu.VMEM((given, SOURCES), jnp.bfloat16)] * 6
        + [pltpu.VMEM((made, width), jnp.float32)],
        compiler_params=pltpu.CompilerParams(vmem_limit_bytes=VMEM_BYTES),
        cost_estimate=pl.CostEstimate(
            flops=2 * 3 * 2 * rows * columns * width,
            bytes_accessed=8 * rows * columns + 4 * width * (rows + columns),
            transcendentals=0,
        ),
    )(kernel, *pieces)


def finish_kernel(count, parts, *refs):
    part_refs, refs = refs[:parts], refs[parts:]
    piece_ref, norm_ref = refs[-2:]
    total = part_refs[0][...]
    for part in part_refs[1:]:
        total = total + part[...]
    norm = jnp.sqrt(total[:1, :1] / count)
    data = total[HEAD:, :] / norm
    if len(refs) > 2:
        other, last_norm = refs[:2]
        data = data - norm * (other[HEAD:, :] / last_norm[:1, :1])
    piece_ref[HEAD:, :] = data
    piece_ref[:HEAD, :] = jnp.broadcast_to(jnp.sum(data * data), (HEAD, data.shape[1]))
    norm_ref[...] = jnp.broadcast_to(norm, norm_ref.shape)


def finish(count, parts, *other):
    shape = parts[0].shape
    return pl.pallas_call(
        functools.partial(finish_kernel, count, len(parts)),
        out_shape=[
            jax.ShapeDtypeStruct(shape, jnp.float32),
            jax.ShapeDtypeStruct((8, 128), jnp.float32),
        ],
        compiler_params=pltpu.CompilerParams(vmem_limit_bytes=SMALL_VMEM_BYTES),
        cost_estimate=pl.CostEstimate(
            flops=shape[0] * shape[1] * 8,
            bytes_accessed=4 * shape[0] * shape[1] * (len(parts) + 2),
            transcendentals=0,
        ),
    )(*parts, *other)


def pack_kernel(slab, place_ref, mark_ref, traces_ref, packed_ref):
    slots, width = packed_ref.shape[0], 2 * SOURCES
    spots = lax.broadcasted_iota(jnp.int32, (place_ref.shape[0], slots), 1)
    chosen = (place_ref[...] == spots).astype(jnp.bfloat16)
    for part in range(2):
        start = (part * FREQS + slab) * SOURCES
        packed_ref[:, part * SOURCES : (part + 1) * SOURCES] = dot_exact(
            chosen, traces_ref[:, start : start + SOURCES]
        )
    if packed_ref.shape[1] > width:
        marks = jnp.broadcast_to(mark_ref[...], (mark_ref.shape[0], LANES))
        packed_ref[:, width:] = dot_exact(chosen, marks)


def unpack_kernel(sources, *refs):
    mark_ref, part_refs, (piece_ref, marks, data) = refs[0], refs[1:-3], refs[-3:]
    slots, width = data.shape
    rows = (piece_ref.shape[0] - HEAD) // CHUNKS
    if sources is None:
        marks[...], data[...] = mark_ref[:, :1], part_refs[0][:, :width]
    else:
        peer = slots // len(sources)
        for index, (part, start, source) in enumerate(sources):
            here = slice(index * peer, (index + 1) * peer)
            marks[here, :] = mark_ref[pl.ds(pl.multiple_of(source() * peer, peer), peer), :1]
            data[here, :] = part_refs[part][start * peer : (start + 1) * peer, :]
    spots = lax.broadcasted_iota(jnp.int32, (slots, rows), 1) + 1
    chosen = (marks[...].astype(jnp.int32) == spots).astype(jnp.bfloat16)
    placed = dot_exact(chosen, data[...])
    for chunk in range(CHUNKS):
        start = HEAD + chunk * rows
        piece_ref[start : start + rows, :] = placed[:, chunk * LANES : (chunk + 1) * LANES]
    piece_ref[:HEAD, :] = jnp.broadcast_to(jnp.sum(placed * placed), (HEAD, LANES))


class Dispatch:
    def __init__(self, traces, acq_lists, counts, row_count):
        self.traces, self.row_count = traces.reshape(traces.shape[1], -1), row_count
        self.areas = lax.axis_size("z") * lax.axis_size("y")
        slot_count = traces.shape[1]
        self.peer = -(-slot_count // self.areas)
        ids = acq_lists[0]
        iota = jnp.arange(slot_count, dtype=jnp.int32)
        self.area = jnp.where(iota < counts[0, 0], ids // row_count, -1)
        before = (self.area[:, None] == self.area[None, :]) & (iota[None, :] < iota[:, None])
        self.rank = jnp.sum(before.astype(jnp.int32), axis=1)
        self.mark = (ids % row_count + 1).astype(jnp.float32)[:, None]

    def pack(self, slab, marked, order):
        place = jnp.where(self.area >= 0, order * self.peer + self.rank, -1)
        width = 2 * SOURCES
        slots = self.areas * self.peer
        return pl.pallas_call(
            functools.partial(pack_kernel, slab),
            out_shape=jax.ShapeDtypeStruct((slots, width + LANES * marked), jnp.float32),
            compiler_params=pltpu.CompilerParams(vmem_limit_bytes=SMALL_VMEM_BYTES),
        )(place[:, None], self.mark, self.traces)

    def exchange(self, slab, marked):
        packed = self.pack(slab, marked, self.area).reshape(self.areas, self.peer, -1)
        packed = lax.all_to_all(packed, REC, 0, 0, tiled=True)
        return packed.reshape(self.areas * self.peer, -1)

    def unpack(self, marks, parts, sources=None):
        slots, width = self.areas * self.peer, 2 * SOURCES
        shape = (HEAD + CHUNKS * self.row_count, LANES)
        return pl.pallas_call(
            functools.partial(unpack_kernel, sources),
            out_shape=jax.ShapeDtypeStruct(shape, jnp.float32),
            scratch_shapes=[
                pltpu.VMEM((slots, 1), jnp.float32),
                pltpu.VMEM((slots, width), jnp.float32),
            ],
            compiler_params=pltpu.CompilerParams(vmem_limit_bytes=SMALL_VMEM_BYTES),
        )(marks, *parts)

    def first(self):
        received = self.exchange(0, True)
        self.marks = received[:, 2 * SOURCES :]
        self.piece = self.unpack(self.marks, [received])
        return self.piece


def swap(values, axis, k=1):
    size = lax.axis_size(axis)
    return lax.ppermute(values, axis, [(i, i ^ k) for i in range(size)])


def at_end():
    index = lax.axis_index("z")
    return (index == 0) | (index == 3)


LATER = "~"
ASKED = {
    "y": lambda values: swap(values, "y"),
    "x": lambda values: swap(values, "x"),
    "c": lambda values: swap(values, "c"),
    "z": lambda values: swap(values, "z"),
    "mid": lambda values: lax.ppermute(values, "z", [(1, 2), (2, 1)]),
    "up": lambda values: swap(values, "z"),
    "down": lambda values: swap(values, "z"),
    "hold": lambda values: values,
}


def answer(asked):
    results = [None] * len(asked)
    asked = [(kind.rstrip(LATER), values) for kind, values in asked]
    kinds = [kind for kind, _ in asked]
    if "up" in kinds and "down" in kinds:
        up, down = kinds.index("up"), kinds.index("down")
        both = jnp.where(at_end(), asked[up][1], asked[down][1])
        results[up] = results[down] = swap(both, "z")
    for kind in ASKED:
        for index, (wanted, values) in enumerate(asked):
            if wanted == kind and results[index] is None:
                results[index] = ASKED[kind](values)
    return results


def line_place(kind):
    index = lax.axis_index("z")
    if kind == "own":
        return index
    if kind == "partner":
        return other("z")
    near = jnp.where(index < 2, 1, 0)
    return 1 + near if kind == "third" else 3 * near


def rec_place(kind, across):
    return lambda: line_place(kind) * 2 + (other("y") if across else lax.axis_index("y"))


def src_place(across_x, across_c):
    return lambda: (other("x") if across_x else lax.axis_index("x")) * 2 + (
        other("c") if across_c else lax.axis_index("c")
    )


def source_place(kz, ky):
    return (lax.axis_index("z") ^ kz) * 2 + (lax.axis_index("y") ^ ky)


KINDS = ("own", "partner", "third", "far")


class Neighbours:
    side = "z"
    rec_outs = [[rec_place(kind, across)] for across in (0, 1) for kind in KINDS]
    src_outs = [[src_place(0, 1), src_place(1, 1)], [src_place(1, 0)], [src_place(0, 0)]]

    def gather_src(self, own):
        x, c = yield ("x", own), ("c", own)
        return [own, x, c, swap(x, "c")], [src_place(*k) for k in ((0, 0), (1, 0), (0, 1), (1, 1))]

    def gather_rec(self, own):
        own_y, partner, mid = yield ("y~", own), ("z", own), ("mid", own)
        third, mid_two, own_y = yield ("down", mid), ("mid", partner), ("hold", own_y)
        third = jnp.where(at_end(), third, mid)
        third_y, far, own_y = yield ("y", third), ("down", mid_two), ("hold", own_y)
        far = jnp.where(at_end(), far, mid_two)
        far_y, partner_y, third_y = yield ("y", far), ("z", own_y), ("hold", third_y)
        return [own, partner, third, far, own_y, partner_y, third_y, far_y], [
            place for (place,) in self.rec_outs
        ]

    def dispatch(self, given, slab, lag):
        z, y = lax.axis_index("z"), lax.axis_index("y")
        apart = (given.area // 2) ^ z, (given.area % 2) ^ y
        packed = given.pack(slab, False, apart[1] * 4 + apart[0])
        packed, _ = lax.optimization_barrier((packed, given.piece))
        peer = given.peer
        (got,) = yield (("y", packed[4 * peer :]),)
        sent = [
            jnp.concatenate([part[k * peer : (k + 1) * peer] for part in (packed, got)])
            for k in range(4)
        ]
        near, far = yield ("z", sent[1]), ("hold", swap(sent[3], "z", 3))
        (middle,) = yield (("hold", swap(sent[2], "z", 2)),)
        for _ in range(lag - 3):
            yield ()
        parts = [far, middle, near]
        sources = [
            (part, start, lambda k=k, start=start: source_place(k, start))
            for part, k in ((0, 0), (1, 3), (2, 2), (3, 1))
            for start in range(2)
        ]
        return given.unpack(given.marks, [sent[0], *parts], sources)

    def scatter_rec(self, blocks):
        blocks = yield tuple(("hold", block) for block in blocks)
        own, partner, third, far, own_y, partner_y, third_y, far_y = blocks
        got_far, got_own_y, third_y, own_y, third = yield (
            ("y", far_y), (self.side, partner_y), ("hold", third_y), ("hold", own_y), ("hold", third),
        )
        far = far + got_far
        got_third, got_far, got_own_y, own_y, third, far = yield (
            ("y", third_y), ("up", far), ("hold", got_own_y), ("hold", own_y), ("hold", third),
            ("hold", far),
        )
        own_y = own_y + got_own_y
        third = third + got_third
        far = far + got_far
        got_own, got_third, got_partner, third = yield (
            ("y~", own_y), ("up", third), ("mid", far), ("hold", third),
        )
        partner = partner + got_partner
        third = third + got_third
        last = yield ("hold", got_own), ("z", partner), ("mid", third)
        return [own, *last]

    def scatter_src(self, blocks):
        sent, across, own = yield tuple(("hold", block) for block in blocks)
        back = swap(sent, "c")
        (far,) = yield (("x", across + back[1]),)
        return [own, back[0], far]


class Whole:
    rec_outs = [[None]]
    src_outs = [[None]]

    def gather(self, piece, axes):
        pieces = lax.all_gather(piece, axes, axis=0, tiled=False)
        data = pieces[:, HEAD:].reshape(pieces.shape[0], CHUNKS, -1, LANES)
        data = data.transpose(1, 0, 2, 3).reshape(-1, LANES)
        return [jnp.concatenate([jnp.sum(pieces[:, :HEAD], axis=0), data], axis=0)], [None]

    def scatter(self, blocks, axes):
        count = lax.axis_size(axes[0]) * lax.axis_size(axes[1])
        head = jnp.broadcast_to(blocks[0][:HEAD], (count, HEAD, LANES))
        data = blocks[0][HEAD:].reshape(CHUNKS, count, -1, LANES)
        data = data.transpose(1, 0, 2, 3).reshape(count, -1, LANES)
        both = jnp.concatenate([head, data], axis=1)
        return [lax.psum_scatter(both, axes, scatter_dimension=0, tiled=False)]

    def dispatch(self, given, slab, lag):
        (received,) = yield (("hold", given.exchange(slab, False)),)
        return given.unpack(given.marks, [received])

    def gather_src(self, piece):
        (piece,) = yield (("hold", piece),)
        return self.gather(piece, SRC)

    def gather_rec(self, piece):
        (piece,) = yield (("hold", piece),)
        return self.gather(piece, REC)

    def scatter_rec(self, blocks):
        (blocks,) = yield (("hold", blocks),)
        return self.scatter(blocks, REC)

    def scatter_src(self, blocks):
        (blocks,) = yield (("hold", blocks),)
        return self.scatter(blocks, SRC)


def global_sum(values):
    for axis in ("c", "x", "y", "z"):
        k = 1
        while k < lax.axis_size(axis):
            values = values + swap(values, axis, 2 * k - 1)
            k *= 2
    return values


LAG = 4


def in_slots(chains):
    values, results = [None] * len(chains), [None] * len(chains)
    live = list(range(len(chains)))
    while live:
        made = {}
        for index in list(live):
            try:
                made[index] = chains[index].send(values[index])
            except StopIteration as stop:
                results[index] = stop.value
                live.remove(index)
        asked = [request for requests in made.values() for request in requests]
        answers = answer(asked)
        waits = [index for index, (kind, _) in enumerate(asked) if not kind.endswith(LATER)]
        closed = lax.optimization_barrier(tuple(answers[index] for index in waits))
        for index, result in zip(waits, closed):
            answers[index] = result
        given = iter(answers)
        for index, requests in made.items():
            values[index] = tuple(next(given) for _ in requests)
    return results


def chain(moves, kernel, slab, given, row_count, column_count, count):
    def adjoint(piece):
        pieces, places = yield from moves.gather_src(piece)
        rows = column_count if len(moves.rec_outs) > 1 else kernel.shape[3]
        blocks = product(kernel, slab, True, pieces, places, moves.rec_outs, rows)
        return (yield from moves.scatter_rec(blocks))

    def forward(piece):
        pieces, places = yield from moves.gather_rec(piece)
        rows = row_count if len(moves.src_outs) > 1 else kernel.shape[2]
        blocks = product(kernel, slab, False, pieces, places, moves.src_outs, rows)
        return (yield from moves.scatter_src(blocks))

    left = given.piece if slab == 0 else (yield from moves.dispatch(given, slab, slab * LAG))
    right, beta = finish(count, (yield from adjoint(left)))
    rights, norms = [], [beta]
    for iteration in range(ITERS):
        left, alpha = finish(count, (yield from forward(right)), left, beta)
        rights.append(right)
        norms.append(alpha)
        if iteration + 1 < ITERS:
            right, beta = finish(count, (yield from adjoint(left)), right, alpha)
            norms.append(beta)
    return rights, norms, left


def put_slab(out, slab, piece):
    rows, each = out.shape[0], CHUNKS // 2
    for chunk in range(CHUNKS):
        at = (chunk // each * FREQS + slab) * SOURCES + chunk % each * LANES
        out[:, at : at + LANES] = piece[chunk * rows : (chunk + 1) * rows, :]


def join_left_kernel(*refs):
    for slab, left in enumerate(refs[:-1]):
        put_slab(refs[-1], slab, left[HEAD:, :])


def join_solution_kernel(count, *refs):
    refs, out = refs[:-1], refs[-1]
    for slab in range(FREQS):
        start = slab * 3 * ITERS
        rights = refs[start : start + ITERS]
        norms = [ref[:1, :1] for ref in refs[start + ITERS : start + 3 * ITERS]]
        norms.append(jnp.sqrt(refs[-1][slab : slab + 1, :1] / count))
        phibar, betas, alphas = norms[0], norms[2::2], norms[1::2]
        for iteration in range(ITERS):
            unit = rights[iteration][HEAD:, :] / alphas[iteration]
            if iteration == 0:
                rhobar, search = alphas[0], unit
            else:
                rhobar = -cosine * alphas[iteration]
                search = unit - (sine * alphas[iteration] / rho) * search
            rho = jnp.sqrt(rhobar * rhobar + betas[iteration] * betas[iteration])
            cosine = rhobar / rho
            sine = betas[iteration] / rho
            phi = cosine * phibar
            phibar = sine * phibar
            step = (phi / rho) * search
            solution = step if iteration == 0 else solution + step
        put_slab(out, slab, solution)


def join(kernel, pieces):
    rows, width = (pieces[0].shape[0] - HEAD) // CHUNKS, 2 * FREQS * SOURCES
    joined = pl.pallas_call(
        kernel,
        out_shape=jax.ShapeDtypeStruct((rows, width), jnp.float32),
        compiler_params=pltpu.CompilerParams(vmem_limit_bytes=SMALL_VMEM_BYTES),
        cost_estimate=pl.CostEstimate(
            flops=rows * width * 4, bytes_accessed=8 * rows * width, transcendentals=0
        ),
    )(*pieces)
    return joined.reshape(rows, 2, FREQS, SOURCES)


def on_device(kernel, traces, acq_lists, counts):
    sizes = tuple(lax.axis_size(axis) for axis in ("z", "y", "x", "c"))
    row_count = kernel.shape[2] // (sizes[2] * sizes[3])
    column_count = kernel.shape[3] // (sizes[0] * sizes[1])
    aligned = row_count % 16 == 0 and column_count % 16 == 0
    moves = Neighbours() if sizes == (4, 2, 2, 2) and aligned else Whole()
    count = 2.0 * kernel.shape[2] * sizes[0] * sizes[1] * SOURCES
    given = Dispatch(traces, acq_lists, counts, row_count)
    given.first()
    chains = [
        chain(moves, kernel, slab, given, row_count, column_count, count)
        for slab in range(FREQS)
    ]
    rights, norms, lefts = zip(*in_slots(chains))
    row = lax.broadcasted_iota(jnp.int32, (HEAD, LANES), 0)
    sums = global_sum(jnp.where(row == 0, lefts[0][:HEAD], lefts[1][:HEAD]))
    given = [ref for pair in zip(rights, norms) for group in pair for ref in group] + [sums]
    return join(functools.partial(join_solution_kernel, count), given), join(
        join_left_kernel, lefts
    )


def solution(mesh):
    rec, src = mesh.shape["rec"], mesh.shape["src"]
    depth = src // 2
    fine = Mesh(
        mesh.devices.reshape(rec // depth, depth, depth, 2), REC + SRC
    )
    placed = (
        P(None, None, REC, SRC),
        P(SRC, REC, None, None, None),
        P(SRC, REC),
        P(SRC, REC),
    )
    return jax.shard_map(
        on_device,
        mesh=fine,
        in_specs=placed,
        out_specs=(P(SRC + REC, None, None, None), P(REC + SRC, None, None, None)),
        check_vma=False,
    )
```

profile of v0, /device:TPU:0, one launch (start us, length us, event | category | flops | bytes accessed | tf_op | source)
XLA Modules:
  0.0 409.4 jit_solution(14256914380286731237)
XLA Ops:
  3.2 2.3 reshape.243.traces_ref
  7.1 28.7 %all_to_all.5 = f32[8,40,640]{2,1,0:T(8,128)S(1)} all-to-all(f32[8,40,640]{2,1,0:T(8,128)S(1)} %bitcast.37), channel_id=1, replica_groups=mesh['z'=4,'y'=2,'x'=2,'c'=2] {'z','y'}, dimensions={0} | all-to-all | bytes 1638400 | tf_op jit(solution)/shard_map/all_to_all | solution.py:229
  39.7 9.4 %collective-permute-done.2 = f32[160,512]{1,0:T(8,128)S(1)} collective-permute-done((f32[160,512]{1,0:T(8,128)S(1)}, f32[160,512]{1,0:T(8,128)S(1)}, u32[]{:S(2)}, u32[]{:S(2)}) %collective-permute-start.2) | collective-permute-done | bytes 327712 | tf_op jit(solution)/shard_map/ppermute | solution.py:254
  50.8 7.6 %shard_map.62 = (f32[648,128]{1,0:T(8,128)S(1)}, f32[648,128]{1,0:T(8,128)S(1)}, f32[648,128]{1,0:T(8,128)S(1)}, f32[648,128]{1,0:T(8,128)S(1)}, f32[648,128]{1,...) custom-call(f32[2,2,640,1280]{3,2,1,0:T(8,128)} %k_ref.15, ...), custom_call_target="tpu_custom_call" | custom-call | flops 5033164800 | bytes 10485760 | tf_op jit(solution)/shard_map/pallas_call | solution.py:118
  58.5 2.1 collective-permute-done.4.refs_4_
  61.6 2.4 collective-permute-start.8
  64.0 7.7 %collective-permute-done.8.refs_3_ = f32[80,512]{1,0:T(8,128)S(1)} collective-permute-done((f32[80,512]{1,0:T(8,128)S(1)}, f32[80,512]{1,0:T(8,128)S(1)}, u32[]{:S(2)}, u32[]{:S(2)}) %collective-permute-start.8) | collective-permute-done | bytes 163872 | tf_op jit(solution)/shard_map/ppermute | solution.py:254
  71.8 1.9 collective-permute-done.7
  78.0 4.1 %collective-permute-done.10 = f32[648,128]{1,0:T(8,128)S(1)} collective-permute-done((f32[648,128]{1,0:T(8,128)S(1)}, f32[648,128]{1,0:T(8,128)S(1)}, u32[]{:S(2)}, u32[]{:S(2)}) %collective-permute-start.10) | collective-permute-done | bytes 331808 | tf_op jit(solution)/shard_map/ppermute | solution.py:254
  84.1 4.0 collective-permute-start.12
  88.1 5.5 %collective-permute-done.12 = f32[648,128]{1,0:T(8,128)S(1)} collective-permute-done((f32[648,128]{1,0:T(8,128)S(1)}, f32[648,128]{1,0:T(8,128)S(1)}, u32[]{:S(2)}, u32[]{:S(2)}) %collective-permute-start.12) | collective-permute-done | bytes 331808 | tf_op jit(solution)/shard_map/ppermute | solution.py:254
  96.0 3.3 collective-permute-start.16
  99.3 8.4 %shard_map.64 = (f32[648,128]{1,0:T(8,128)S(1)}, f32[648,128]{1,0:T(8,128)S(1)}, f32[648,128]{1,0:T(8,128)S(1)}, f32[648,128]{1,0:T(8,128)S(1)}, f32[648,128]{1,...) custom-call(f32[2,2,640,1280]{3,2,1,0:T(8,128)} %k_ref.15, ...), custom_call_target="tpu_custom_call" | custom-call | flops 5033164800 | bytes 10485760 | tf_op jit(solution)/shard_map/pallas_call | solution.py:118
  111.5 3.4 collective-permute-start.22
  116.2 3.1 collective-permute-done.19.refs_1_
  119.3 2.5 collective-permute-done.21
  121.8 3.2 collective-permute-done.22
  128.1 6.6 %collective-permute-done.23 = f32[648,128]{1,0:T(8,128)S(1)} collective-permute-done((f32[648,128]{1,0:T(8,128)S(1)}, f32[648,128]{1,0:T(8,128)S(1)}, u32[]{:S(2)}, u32[]{:S(2)}) %collective-permute-start.23) | collective-permute-done | bytes 331808 | tf_op jit(solution)/shard_map/ppermute | solution.py:254
  136.3 6.1 %collective-permute-start.28 = (f32[648,128]{1,0:T(8,128)S(1)}, f32[648,128]{1,0:T(8,128)S(1)}, u32[]{:S(2)}, u32[]{:S(2)}) collective-permute-start(f32[648,128]{1,0:T(8,128)S(1)} %get-tuple-element.466), channel_id=1, source_target_pairs={{0,8},{8,0},{16,24},{24,16},{1,9},{9,1},{17,25},{25,17},{2,10},{10... | collective-permute-start | bytes 995336 | tf_op jit(solution)/shard_map/ppermute | solution.py:254
  145.6 2.0 collective-permute-done.28
  147.6 5.2 %collective-permute-done.27.refs_6_ = f32[648,128]{1,0:T(8,128)S(1)} collective-permute-done((f32[648,128]{1,0:T(8,128)S(1)}, f32[648,128]{1,0:T(8,128)S(1)}, u32[]{:S(2)}, u32[]{:S(2)}) %collective-permute-start.27) | collective-permute-done | bytes 331808 | tf_op jit(solution)/shard_map/ppermute | solution.py:254
  153.6 4.3 %collective-permute-start.33 = (f32[648,128]{1,0:T(8,128)S(1)}, f32[648,128]{1,0:T(8,128)S(1)}, u32[]{:S(2)}, u32[]{:S(2)}) collective-permute-start(f32[648,128]{1,0:T(8,128)S(1)} %add.204), channel_id=1, source_target_pairs={{0,8},{8,0},{16,24},{24,16},{1,9},{9,1},{17,25},{25,17},{2,10},{10... | collective-permute-start | bytes 995336 | tf_op jit(solution)/shard_map/ppermute | solution.py:254
  159.8 3.6 collective-permute-done.33.refs_2_
  165.1 5.0 %collective-permute-done.31.refs_5_ = f32[648,128]{1,0:T(8,128)S(1)} collective-permute-done((f32[648,128]{1,0:T(8,128)S(1)}, f32[648,128]{1,0:T(8,128)S(1)}, u32[]{:S(2)}, u32[]{:S(2)}) %collective-permute-start.31) | collective-permute-done | bytes 331808 | tf_op jit(solution)/shard_map/ppermute | solution.py:254
  170.5 2.1 collective-permute-start.35
  173.2 7.0 %shard_map.66 = (f32[2,648,128]{2,1,0:T(8,128)S(1)}, f32[648,128]{1,0:T(8,128)S(1)}, f32[648,128]{1,0:T(8,128)S(1)}) custom-call(f32[2,2,640,1280]{3,2,1,0:T(8,128)} %k_ref.15, f32[648,128]{1,0:T(8,128)S(1)} %get-tuple-element.281.refs_0_.refs_4_, f32[648,128]{1,0:T(8,128)} %collective-permute-done.19.refs_1_, ...), custom_call_target="tpu_custom_call" | custom-call | flops 5033164800 | bytes 10485760 | tf_op jit(solution)/shard_map/pallas_call | solution.py:118
  184.4 6.2 %collective-permute-done.41.refs_4_ = f32[648,128]{1,0:T(8,128)S(1)} collective-permute-done((f32[648,128]{1,0:T(8,128)S(1)}, f32[648,128]{1,0:T(8,128)S(1)}, u32[]{:S(2)}, u32[]{:S(2)}) %collective-permute-start.41) | collective-permute-done | bytes 331808 | tf_op jit(solution)/shard_map/ppermute | solution.py:254
  191.0 2.4 collective-permute-done.38.refs_2_
  195.8 2.9 collective-permute-start.45
  198.7 3.6 collective-permute-done.44.refs_6_
  203.7 3.4 collective-permute-done.45
  209.7 7.6 %shard_map.69 = (f32[648,128]{1,0:T(8,128)S(1)}, f32[648,128]{1,0:T(8,128)S(1)}, f32[648,128]{1,0:T(8,128)S(1)}, f32[648,128]{1,0:T(8,128)S(1)}, f32[648,128]{1,...) custom-call(f32[2,2,640,1280]{3,2,1,0:T(8,128)} %k_ref.15, ...), custom_call_target="tpu_custom_call" | custom-call | flops 5033164800 | bytes 10485760 | tf_op jit(solution)/shard_map/pallas_call | solution.py:118
  220.9 7.1 %shard_map.70 = (f32[2,648,128]{2,1,0:T(8,128)S(1)}, f32[648,128]{1,0:T(8,128)S(1)}, f32[648,128]{1,0:T(8,128)S(1)}) custom-call(f32[2,2,640,1280]{3,2,1,0:T(8,128)} %k_ref.15, f32[648,128]{1,0:T(8,128)S(1)} %get-tuple-element.321.refs_0_.refs_4_.refs_6_, f32[648,128]{1,0:T(8,128)S(1)} %collective-permute-done.35.refs_1_, ...), custom_call_target="tpu_custom_call" | custom-call | flops 5033164800 | bytes 10485760 | tf_op jit(solution)/shard_map/pallas_call | solution.py:118
  232.2 6.3 %collective-permute-done.52 = f32[648,128]{1,0:T(8,128)S(1)} collective-permute-done((f32[648,128]{1,0:T(8,128)S(1)}, f32[648,128]{1,0:T(8,128)S(1)}, u32[]{:S(2)}, u32[]{:S(2)}) %collective-permute-start.52) | collective-permute-done | bytes 331808 | tf_op jit(solution)/shard_map/ppermute | solution.py:254
  243.1 3.3 collective-permute-start.56
  246.3 3.3 collective-permute-done.58.refs_1_
  249.6 4.9 %collective-permute-done.56 = f32[648,128]{1,0:T(8,128)S(1)} collective-permute-done((f32[648,128]{1,0:T(8,128)S(1)}, f32[648,128]{1,0:T(8,128)S(1)}, u32[]{:S(2)}, u32[]{:S(2)}) %collective-permute-start.56) | collective-permute-done | bytes 331808 | tf_op jit(solution)/shard_map/ppermute | solution.py:254
  256.1 4.6 %collective-permute-start.60 = (f32[648,128]{1,0:T(8,128)S(1)}, f32[648,128]{1,0:T(8,128)S(1)}, u32[]{:S(2)}, u32[]{:S(2)}) collective-permute-start(f32[648,128]{1,0:T(8,128)S(1)} %add.212), channel_id=1, source_target_pairs={{0,8},{8,0},{16,24},{24,16},{1,9},{9,1},{17,25},{25,17},{2,10},{10... | collective-permute-start | bytes 995336 | tf_op jit(solution)/shard_map/ppermute | solution.py:254
  260.7 7.6 %shard_map.72 = (f32[648,128]{1,0:T(8,128)S(1)}, f32[648,128]{1,0:T(8,128)S(1)}, f32[648,128]{1,0:T(8,128)S(1)}, f32[648,128]{1,0:T(8,128)S(1)}, f32[648,128]{1,...) custom-call(f32[2,2,640,1280]{3,2,1,0:T(8,128)} %k_ref.15, ...), custom_call_target="tpu_custom_call" | custom-call | flops 5033164800 | bytes 10485760 | tf_op jit(solution)/shard_map/pallas_call | solution.py:118
  272.9 2.0 collective-permute-start.66
  275.6 4.2 %collective-permute-done.63.refs_1_ = f32[648,128]{1,0:T(8,128)S(1)} collective-permute-done((f32[648,128]{1,0:T(8,128)S(1)}, f32[648,128]{1,0:T(8,128)S(1)}, u32[]{:S(2)}, u32[]{:S(2)}) %collective-permute-start.63) | collective-permute-done | bytes 331808 | tf_op jit(solution)/shard_map/ppermute | solution.py:254
  279.8 2.5 collective-permute-done.65
  282.3 3.0 collective-permute-done.66
  288.9 4.7 %collective-permute-done.67 = f32[648,128]{1,0:T(8,128)S(1)} collective-permute-done((f32[648,128]{1,0:T(8,128)S(1)}, f32[648,128]{1,0:T(8,128)S(1)}, u32[]{:S(2)}, u32[]{:S(2)}) %collective-permute-start.67) | collective-permute-done | bytes 331808 | tf_op jit(solution)/shard_map/ppermute | solution.py:254
  296.2 5.2 %collective-permute-start.72 = (f32[648,128]{1,0:T(8,128)S(1)}, f32[648,128]{1,0:T(8,128)S(1)}, u32[]{:S(2)}, u32[]{:S(2)}) collective-permute-start(f32[648,128]{1,0:T(8,128)S(1)} %get-tuple-element.462), channel_id=1, source_target_pairs={{0,8},{8,0},{16,24},{24,16},{1,9},{9,1},{17,25},{25,17},{2,10},{10... | collective-permute-start | bytes 995336 | tf_op jit(solution)/shard_map/ppermute | solution.py:254
  303.7 2.8 collective-permute-done.72
  306.5 5.7 %collective-permute-done.71.refs_6_ = f32[648,128]{1,0:T(8,128)S(1)} collective-permute-done((f32[648,128]{1,0:T(8,128)S(1)}, f32[648,128]{1,0:T(8,128)S(1)}, u32[]{:S(2)}, u32[]{:S(2)}) %collective-permute-start.71) | collective-permute-done | bytes 331808 | tf_op jit(solution)/shard_map/ppermute | solution.py:254
  318.4 1.9 collective-permute-done.77.refs_2_
  322.1 4.9 %collective-permute-done.75.refs_5_ = f32[648,128]{1,0:T(8,128)S(1)} collective-permute-done((f32[648,128]{1,0:T(8,128)S(1)}, f32[648,128]{1,0:T(8,128)S(1)}, u32[]{:S(2)}, u32[]{:S(2)}) %collective-permute-start.75) | collective-permute-done | bytes 331808 | tf_op jit(solution)/shard_map/ppermute | solution.py:254
  327.4 2.2 collective-permute-start.79
  330.3 7.2 %shard_map.74 = (f32[2,648,128]{2,1,0:T(8,128)S(1)}, f32[648,128]{1,0:T(8,128)S(1)}, f32[648,128]{1,0:T(8,128)S(1)}) custom-call(f32[2,2,640,1280]{3,2,1,0:T(8,128)} %k_ref.15, f32[648,128]{1,0:T(8,128)S(1)} %get-tuple-element.394.refs_0_.refs_1_, f32[648,128]{1,0:T(8,128)S(1)} %collective-permute-done.63.refs_1_, ...), custom_call_target="tpu_custom_call" | custom-call | flops 5033164800 | bytes 10485760 | tf_op jit(solution)/shard_map/pallas_call | solution.py:118
  338.9 2.8 collective-permute-start.83
  343.0 4.7 %collective-permute-done.85.refs_4_ = f32[648,128]{1,0:T(8,128)S(1)} collective-permute-done((f32[648,128]{1,0:T(8,128)S(1)}, f32[648,128]{1,0:T(8,128)S(1)}, u32[]{:S(2)}, u32[]{:S(2)}) %collective-permute-start.85) | collective-permute-done | bytes 331808 | tf_op jit(solution)/shard_map/ppermute | solution.py:254
  347.8 2.1 collective-permute-done.83
  349.8 2.3 collective-permute-done.82.refs_2_
  354.6 6.3 %collective-permute-done.86.refs_6_ = f32[648,128]{1,0:T(8,128)S(1)} collective-permute-done((f32[648,128]{1,0:T(8,128)S(1)}, f32[648,128]{1,0:T(8,128)S(1)}, u32[]{:S(2)}, u32[]{:S(2)}) %collective-permute-start.86) | collective-permute-done | bytes 331808 | tf_op jit(solution)/shard_map/ppermute | solution.py:254
  364.5 4.5 %collective-permute-done.88.refs_7_ = f32[648,128]{1,0:T(8,128)S(1)} collective-permute-done((f32[648,128]{1,0:T(8,128)S(1)}, f32[648,128]{1,0:T(8,128)S(1)}, u32[]{:S(2)}, u32[]{:S(2)}) %collective-permute-start.88) | collective-permute-done | bytes 331808 | tf_op jit(solution)/shard_map/ppermute | solution.py:254
  370.0 7.1 %shard_map.77 = (f32[2,648,128]{2,1,0:T(8,128)S(1)}, f32[648,128]{1,0:T(8,128)S(1)}, f32[648,128]{1,0:T(8,128)S(1)}) custom-call(f32[2,2,640,1280]{3,2,1,0:T(8,128)} %k_ref.15, f32[648,128]{1,0:T(8,128)S(1)} %get-tuple-element.436.refs_0_.refs_7_, f32[648,128]{1,0:T(8,128)S(1)} %collective-permute-done.79.refs_1_, ...), custom_call_target="tpu_custom_call" | custom-call | flops 5033164800 | bytes 10485760 | tf_op jit(solution)/shard_map/pallas_call | solution.py:118
  377.3 2.1 collective-permute-done.90
  380.4 8.9 %collective-permute-done.91.refs_2_ = f32[648,128]{1,0:T(8,128)S(1)} collective-permute-done((f32[648,128]{1,0:T(8,128)S(1)}, f32[648,128]{1,0:T(8,128)S(1)}, u32[]{:S(2)}, u32[]{:S(2)}) %collective-permute-start.91) | collective-permute-done | bytes 331808 | tf_op jit(solution)/shard_map/ppermute | solution.py:254
  391.5 3.1 collective-permute-done.93
  395.3 2.9 collective-permute-done.94
  399.8 2.0 collective-permute-done.95
  401.8 2.7 collective-permute-start.96
  (223 shorter events, 104.3 us)
Async XLA Ops:
  36.5 12.6 %collective-permute-start = (f32[648,128]{1,0:T(8,128)S(1)}, f32[648,128]{1,0:T(8,128)S(1)}, u32[]{:S(2)}, u32[]{:S(2)}) collective-permute-start(f32[648,128]{1,0:T(8,128)S(1)} %shard_map.60.refs_0_.refs_3_), channel_id=1, source_target_pairs={{0,2},{2,0},{1,3},{3,1},{4,6},{6,4},{5,7},{7,5},{8,10},{10,8},{9,1... | collective-permute-start | bytes 995336 | tf_op jit(solution)/shard_map/ppermute | solution.py:254
  38.1 11.1 %collective-permute-start.1 = (f32[648,128]{1,0:T(8,128)S(1)}, f32[648,128]{1,0:T(8,128)S(1)}, u32[]{:S(2)}, u32[]{:S(2)}) collective-permute-start(f32[648,128]{1,0:T(8,128)S(1)} %shard_map.60.refs_0_.refs_3_), channel_id=1, source_target_pairs={{0,1},{1,0},{2,3},{3,2},{4,5},{5,4},{6,7},{7,6},{8,9},{9,8},{10,11... | collective-permute-start | bytes 995336 | tf_op jit(solution)/shard_map/ppermute | solution.py:254
  39.0 10.2 %collective-permute-start.2 = (f32[160,512]{1,0:T(8,128)S(1)}, f32[160,512]{1,0:T(8,128)S(1)}, u32[]{:S(2)}, u32[]{:S(2)}) collective-permute-start(f32[160,512]{1,0:T(8,128)S(1)} %slice.61), channel_id=1, source_target_pairs={{0,4},{4,0},{1,5},{5,1},{2,6},{6,2},{3,7},{7,3},{8,12},{12,8},{9,1... | collective-permute-start | bytes 983048 | tf_op jit(solution)/shard_map/ppermute | solution.py:254
  49.2 9.2 %collective-permute-start.5 = (f32[80,512]{1,0:T(8,128)S(1)}, f32[80,512]{1,0:T(8,128)S(1)}, u32[]{:S(2)}, u32[]{:S(2)}) collective-permute-start(f32[80,512]{1,0:T(8,128)S(1)} %pad_maximum_fusion.1), channel_id=1, source_target_pairs={{0,24},{8,16},{16,8},{24,0},{1,25},{9,17},{17,9},{25,1},{2,26},{10... | collective-permute-start | bytes 491528 | tf_op jit(solution)/shard_map/ppermute | solution.py:254
  50.7 9.9 %collective-permute-start.4 = (f32[80,512]{1,0:T(8,128)S(1)}, f32[80,512]{1,0:T(8,128)S(1)}, u32[]{:S(2)}, u32[]{:S(2)}) collective-permute-start(f32[80,512]{1,0:T(8,128)S(1)} %pad_maximum_fusion), channel_id=1, source_target_pairs={{0,8},{8,0},{16,24},{24,16},{1,9},{9,1},{17,25},{25,17},{2,10},{10... | collective-permute-start | bytes 491528 | tf_op jit(solution)/shard_map/ppermute | solution.py:254
  60.6 11.1 %collective-permute-start.6 = (f32[648,128]{1,0:T(8,128)S(1)}, f32[648,128]{1,0:T(8,128)S(1)}, u32[]{:S(2)}, u32[]{:S(2)}) collective-permute-start(f32[648,128]{1,0:T(8,128)S(1)} %get-tuple-element.244), channel_id=1, source_target_pairs={{0,4},{4,0},{1,5},{5,1},{2,6},{6,2},{3,7},{7,3},{8,12},{12,8},{9,1... | collective-permute-start | bytes 995336 | tf_op jit(solution)/shard_map/ppermute | solution.py:254
  61.3 12.4 %collective-permute-start.7 = (f32[648,128]{1,0:T(8,128)S(1)}, f32[648,128]{1,0:T(8,128)S(1)}, u32[]{:S(2)}, u32[]{:S(2)}) collective-permute-start(f32[648,128]{1,0:T(8,128)S(1)} %get-tuple-element.245), channel_id=1, source_target_pairs={{0,8},{8,0},{16,24},{24,16},{1,9},{9,1},{17,25},{25,17},{2,10},{10... | collective-permute-start | bytes 995336 | tf_op jit(solution)/shard_map/ppermute | solution.py:254
  61.6 10.2 %collective-permute-start.8 = (f32[80,512]{1,0:T(8,128)S(1)}, f32[80,512]{1,0:T(8,128)S(1)}, u32[]{:S(2)}, u32[]{:S(2)}) collective-permute-start(f32[80,512]{1,0:T(8,128)S(1)} %pad_maximum_fusion.2), channel_id=1, source_target_pairs={{0,16},{8,24},{16,0},{24,8},{1,17},{9,25},{17,1},{25,9},{2,18},{10... | collective-permute-start | bytes 491528 | tf_op jit(solution)/shard_map/ppermute | solution.py:254
  73.7 8.4 %collective-permute-start.10 = (f32[648,128]{1,0:T(8,128)S(1)}, f32[648,128]{1,0:T(8,128)S(1)}, u32[]{:S(2)}, u32[]{:S(2)}) collective-permute-start(f32[648,128]{1,0:T(8,128)S(1)} %add.194), channel_id=1, source_target_pairs={{0,8},{8,0},{16,24},{24,16},{1,9},{9,1},{17,25},{25,17},{2,10},{10... | collective-permute-start | bytes 995336 | tf_op jit(solution)/shard_map/ppermute | solution.py:254
  77.4 10.7 %collective-permute-start.14 = (f32[648,128]{1,0:T(8,128)S(1)}, f32[648,128]{1,0:T(8,128)S(1)}, u32[]{:S(2)}, u32[]{:S(2)}) collective-permute-start(f32[648,128]{1,0:T(8,128)S(1)} %shard_map.63.refs_0_.refs_3_), channel_id=1, source_target_pairs={{0,2},{2,0},{1,3},{3,1},{4,6},{6,4},{5,7},{7,5},{8,10},{10,8},{9,1... | collective-permute-start | bytes 995336 | tf_op jit(solution)/shard_map/ppermute | solution.py:254
  78.0 10.1 %collective-permute-start.15 = (f32[648,128]{1,0:T(8,128)S(1)}, f32[648,128]{1,0:T(8,128)S(1)}, u32[]{:S(2)}, u32[]{:S(2)}) collective-permute-start(f32[648,128]{1,0:T(8,128)S(1)} %shard_map.63.refs_0_.refs_3_), channel_id=1, source_target_pairs={{0,1},{1,0},{2,3},{3,2},{4,5},{5,4},{6,7},{7,6},{8,9},{9,8},{10,11... | collective-permute-start | bytes 995336 | tf_op jit(solution)/shard_map/ppermute | solution.py:254
  84.1 9.5 %collective-permute-start.12 = (f32[648,128]{1,0:T(8,128)S(1)}, f32[648,128]{1,0:T(8,128)S(1)}, u32[]{:S(2)}, u32[]{:S(2)}) collective-permute-start(f32[648,128]{1,0:T(8,128)S(1)} %add.196), channel_id=1, source_target_pairs={{0,8},{8,0},{16,24},{24,16},{1,9},{9,1},{17,25},{25,17},{2,10},{10... | collective-permute-start | bytes 995336 | tf_op jit(solution)/shard_map/ppermute | solution.py:254
  93.6 14.1 %collective-permute-start.11 = (f32[648,128]{1,0:T(8,128)S(1)}, f32[648,128]{1,0:T(8,128)S(1)}, u32[]{:S(2)}, u32[]{:S(2)}) collective-permute-start(f32[648,128]{1,0:T(8,128)S(1)} %add.195), channel_id=1, source_target_pairs={{0,4},{4,0},{1,5},{5,1},{2,6},{6,2},{3,7},{7,3},{8,12},{12,8},{9,1... | collective-permute-start | bytes 995336 | tf_op jit(solution)/shard_map/ppermute | solution.py:254
  95.1 12.7 %collective-permute-start.17 = (f32[648,128]{1,0:T(8,128)S(1)}, f32[648,128]{1,0:T(8,128)S(1)}, u32[]{:S(2)}, u32[]{:S(2)}) collective-permute-start(f32[648,128]{1,0:T(8,128)S(1)} %add.199), channel_id=1, source_target_pairs={{8,16},{16,8},{9,17},{17,9},{10,18},{18,10},{11,19},{19,11},{12,20... | collective-permute-start | bytes 995336 | tf_op jit(solution)/shard_map/ppermute | solution.py:268
  96.0 11.8 %collective-permute-start.16 = (f32[648,128]{1,0:T(8,128)S(1)}, f32[648,128]{1,0:T(8,128)S(1)}, u32[]{:S(2)}, u32[]{:S(2)}) collective-permute-start(f32[648,128]{1,0:T(8,128)S(1)} %add.198), channel_id=1, source_target_pairs={{0,8},{8,0},{16,24},{24,16},{1,9},{9,1},{17,25},{25,17},{2,10},{10... | collective-permute-start | bytes 995336 | tf_op jit(solution)/shard_map/ppermute | solution.py:254
  108.5 10.8 %collective-permute-start.19 = (f32[648,128]{1,0:T(8,128)S(1)}, f32[648,128]{1,0:T(8,128)}, u32[]{:S(2)}, u32[]{:S(2)}) collective-permute-start(f32[648,128]{1,0:T(8,128)S(1)} %get-tuple-element.281.refs_0_.refs_4_), channel_id=1, source_target_pairs={{0,8},{8,0},{16,24},{24,16},{1,9},{9,1},{17,25},{25,17},{2,10},{10... | collective-permute-start | bytes 995336 | tf_op jit(solution)/shard_map/ppermute | solution.py:254
  109.4 9.9 %collective-permute-start.20 = (f32[648,128]{1,0:T(8,128)S(1)}, f32[648,128]{1,0:T(8,128)}, u32[]{:S(2)}, u32[]{:S(2)}) collective-permute-start(f32[648,128]{1,0:T(8,128)S(1)} %get-tuple-element.281.refs_0_.refs_4_), channel_id=1, source_target_pairs={{8,16},{16,8},{9,17},{17,9},{10,18},{18,10},{11,19},{19,11},{12,20... | collective-permute-start | bytes 995336 | tf_op jit(solution)/shard_map/ppermute | solution.py:268
  110.8 11.1 %collective-permute-start.21 = (f32[648,128]{1,0:T(8,128)}, f32[648,128]{1,0:T(8,128)}, u32[]{:S(2)}, u32[]{:S(2)}) collective-permute-start(f32[648,128]{1,0:T(8,128)} %get-tuple-element.282), channel_id=1, source_target_pairs={{0,4},{4,0},{1,5},{5,1},{2,6},{6,2},{3,7},{7,3},{8,12},{12,8},{9,1... | collective-permute-start | bytes 995336 | tf_op jit(solution)/shard_map/ppermute | solution.py:254
  111.5 13.6 %collective-permute-start.22 = (f32[648,128]{1,0:T(8,128)}, f32[648,128]{1,0:T(8,128)}, u32[]{:S(2)}, u32[]{:S(2)}) collective-permute-start(f32[648,128]{1,0:T(8,128)} %get-tuple-element.283), channel_id=1, source_target_pairs={{0,8},{8,0},{16,24},{24,16},{1,9},{9,1},{17,25},{25,17},{2,10},{10... | collective-permute-start | bytes 995336 | tf_op jit(solution)/shard_map/ppermute | solution.py:254
  114.9 13.2 %collective-permute-start.25 = (f32[648,128]{1,0:T(8,128)S(1)}, f32[648,128]{1,0:T(8,128)S(1)}, u32[]{:S(2)}, u32[]{:S(2)}) collective-permute-start(f32[648,128]{1,0:T(8,128)S(1)} %get-tuple-element.281.refs_0_.refs_4_), channel_id=1, source_target_pairs={{0,4},{4,0},{1,5},{5,1},{2,6},{6,2},{3,7},{7,3},{8,12},{12,8},{9,1... | collective-permute-start | bytes 995336 | tf_op jit(solution)/shard_map/ppermute | solution.py:254
  126.1 8.5 %collective-permute-start.23 = (f32[648,128]{1,0:T(8,128)S(1)}, f32[648,128]{1,0:T(8,128)S(1)}, u32[]{:S(2)}, u32[]{:S(2)}) collective-permute-start(f32[648,128]{1,0:T(8,128)S(1)} %get-tuple-element.468), channel_id=1, source_target_pairs={{0,8},{8,0},{16,24},{24,16},{1,9},{9,1},{17,25},{25,17},{2,10},{10... | collective-permute-start | bytes 995336 | tf_op jit(solution)/shard_map/ppermute | solution.py:254
  135.5 10.1 %collective-permute-start.29 = (f32[648,128]{1,0:T(8,128)S(1)}, f32[648,128]{1,0:T(8,128)S(1)}, u32[]{:S(2)}, u32[]{:S(2)}) collective-permute-start(f32[648,128]{1,0:T(8,128)S(1)} %add.202), channel_id=1, source_target_pairs={{8,16},{16,8},{9,17},{17,9},{10,18},{18,10},{11,19},{19,11},{12,20... | collective-permute-start | bytes 995336 | tf_op jit(solution)/shard_map/ppermute | solution.py:268
  136.3 11.3 %collective-permute-start.28 = (f32[648,128]{1,0:T(8,128)S(1)}, f32[648,128]{1,0:T(8,128)S(1)}, u32[]{:S(2)}, u32[]{:S(2)}) collective-permute-start(f32[648,128]{1,0:T(8,128)S(1)} %get-tuple-element.466), channel_id=1, source_target_pairs={{0,8},{8,0},{16,24},{24,16},{1,9},{9,1},{17,25},{25,17},{2,10},{10... | collective-permute-start | bytes 995336 | tf_op jit(solution)/shard_map/ppermute | solution.py:254
  142.4 10.4 %collective-permute-start.27 = (f32[648,128]{1,0:T(8,128)S(1)}, f32[648,128]{1,0:T(8,128)S(1)}, u32[]{:S(2)}, u32[]{:S(2)}) collective-permute-start(f32[648,128]{1,0:T(8,128)S(1)} %broadcast_select_fusion.10.refs_2_), channel_id=1, source_target_pairs={{0,4},{4,0},{1,5},{5,1},{2,6},{6,2},{3,7},{7,3},{8,12},{12,8},{9,1... | collective-permute-start | bytes 995336 | tf_op jit(solution)/shard_map/ppermute | solution.py:254
  144.2 15.7 %collective-permute-start.32 = (f32[648,128]{1,0:T(8,128)S(1)}, f32[648,128]{1,0:T(8,128)S(1)}, u32[]{:S(2)}, u32[]{:S(2)}) collective-permute-start(f32[648,128]{1,0:T(8,128)S(1)} %add.203), channel_id=1, source_target_pairs={{0,4},{4,0},{1,5},{5,1},{2,6},{6,2},{3,7},{7,3},{8,12},{12,8},{9,1... | collective-permute-start | bytes 995336 | tf_op jit(solution)/shard_map/ppermute | solution.py:254
  153.6 9.8 %collective-permute-start.33 = (f32[648,128]{1,0:T(8,128)S(1)}, f32[648,128]{1,0:T(8,128)S(1)}, u32[]{:S(2)}, u32[]{:S(2)}) collective-permute-start(f32[648,128]{1,0:T(8,128)S(1)} %add.204), channel_id=1, source_target_pairs={{0,8},{8,0},{16,24},{24,16},{1,9},{9,1},{17,25},{25,17},{2,10},{10... | collective-permute-start | bytes 995336 | tf_op jit(solution)/shard_map/ppermute | solution.py:254
  158.7 11.4 %collective-permute-start.31 = (f32[648,128]{1,0:T(8,128)S(1)}, f32[648,128]{1,0:T(8,128)S(1)}, u32[]{:S(2)}, u32[]{:S(2)}) collective-permute-start(f32[648,128]{1,0:T(8,128)S(1)} %collective-permute-done.25.refs_4_), channel_id=1, source_target_pairs={{0,8},{8,0},{16,24},{24,16},{1,9},{9,1},{17,25},{25,17},{2,10},{10... | collective-permute-start | bytes 995336 | tf_op jit(solution)/shard_map/ppermute | solution.py:254
  170.5 9.8 %collective-permute-start.35 = (f32[648,128]{1,0:T(8,128)S(1)}, f32[648,128]{1,0:T(8,128)S(1)}, u32[]{:S(2)}, u32[]{:S(2)}) collective-permute-start(f32[648,128]{1,0:T(8,128)S(1)} %get-tuple-element.321.refs_0_.refs_4_.refs_6_), channel_id=1, source_target_pairs={{0,8},{8,0},{16,24},{24,16},{1,9},{9,1},{17,25},{25,17},{2,10},{10... | collective-permute-start | bytes 995336 | tf_op jit(solution)/shard_map/ppermute | solution.py:254
  180.4 10.2 %collective-permute-start.41 = (f32[648,128]{1,0:T(8,128)S(1)}, f32[648,128]{1,0:T(8,128)S(1)}, u32[]{:S(2)}, u32[]{:S(2)}) collective-permute-start(f32[648,128]{1,0:T(8,128)S(1)} %get-tuple-element.321.refs_0_.refs_4_.refs_6_), channel_id=1, source_target_pairs={{0,4},{4,0},{1,5},{5,1},{2,6},{6,2},{3,7},{7,3},{8,12},{12,8},{9,1... | collective-permute-start | bytes 995336 | tf_op jit(solution)/shard_map/ppermute | solution.py:254
  181.1 9.9 %collective-permute-start.39 = (f32[648,128]{1,0:T(8,128)S(1)}, f32[648,128]{1,0:T(8,128)S(1)}, u32[]{:S(2)}, u32[]{:S(2)}) collective-permute-start(f32[648,128]{1,0:T(8,128)S(1)} %collective-permute-done.36), channel_id=1, source_target_pairs={{0,8},{8,0},{16,24},{24,16},{1,9},{9,1},{17,25},{25,17},{2,10},{10... | collective-permute-start | bytes 995336 | tf_op jit(solution)/shard_map/ppermute | solution.py:254
  183.7 9.7 %collective-permute-start.38 = (f32[648,128]{1,0:T(8,128)S(1)}, f32[648,128]{1,0:T(8,128)S(1)}, u32[]{:S(2)}, u32[]{:S(2)}) collective-permute-start(f32[648,128]{1,0:T(8,128)S(1)} %fusion.4), channel_id=1, source_target_pairs={{0,2},{2,0},{1,3},{3,1},{4,6},{6,4},{5,7},{7,5},{8,10},{10,8},{9,1... | collective-permute-start | bytes 995336 | tf_op jit(solution)/shard_map/ppermute | solution.py:254
  193.4 8.8 %collective-permute-start.44 = (f32[648,128]{1,0:T(8,128)S(1)}, f32[648,128]{1,0:T(8,128)S(1)}, u32[]{:S(2)}, u32[]{:S(2)}) collective-permute-start(f32[648,128]{1,0:T(8,128)S(1)} %broadcast_select_fusion.7.refs_2_), channel_id=1, source_target_pairs={{0,4},{4,0},{1,5},{5,1},{2,6},{6,2},{3,7},{7,3},{8,12},{12,8},{9,1... | collective-permute-start | bytes 995336 | tf_op jit(solution)/shard_map/ppermute | solution.py:254
  195.2 8.5 %collective-permute-start.42 = (f32[648,128]{1,0:T(8,128)S(1)}, f32[648,128]{1,0:T(8,128)S(1)}, u32[]{:S(2)}, u32[]{:S(2)}) collective-permute-start(f32[648,128]{1,0:T(8,128)S(1)} %get-tuple-element.329.refs_0_.refs_3_), channel_id=1, source_target_pairs={{0,2},{2,0},{1,3},{3,1},{4,6},{6,4},{5,7},{7,5},{8,10},{10,8},{9,1... | collective-permute-start | bytes 995336 | tf_op jit(solution)/shard_map/ppermute | solution.py:254
  195.8 11.3 %collective-permute-start.45 = (f32[648,128]{1,0:T(8,128)S(1)}, f32[648,128]{1,0:T(8,128)S(1)}, u32[]{:S(2)}, u32[]{:S(2)}) collective-permute-start(f32[648,128]{1,0:T(8,128)S(1)} %collective-permute-done.40), channel_id=1, source_target_pairs={{0,8},{8,0},{16,24},{24,16},{1,9},{9,1},{17,25},{25,17},{2,10},{10... | collective-permute-start | bytes 995336 | tf_op jit(solution)/shard_map/ppermute | solution.py:254
  207.2 10.3 %collective-permute-start.47 = (f32[648,128]{1,0:T(8,128)S(1)}, f32[648,128]{1,0:T(8,128)S(1)}, u32[]{:S(2)}, u32[]{:S(2)}) collective-permute-start(f32[648,128]{1,0:T(8,128)S(1)} %broadcast_select_fusion.6.refs_3_), channel_id=1, source_target_pairs={{0,4},{4,0},{1,5},{5,1},{2,6},{6,2},{3,7},{7,3},{8,12},{12,8},{9,1... | collective-permute-start | bytes 995336 | tf_op jit(solution)/shard_map/ppermute | solution.py:254
  207.9 9.9 %collective-permute-start.48 = (f32[648,128]{1,0:T(8,128)S(1)}, f32[648,128]{1,0:T(8,128)S(1)}, u32[]{:S(2)}, u32[]{:S(2)}) collective-permute-start(f32[648,128]{1,0:T(8,128)S(1)} %collective-permute-done.41.refs_4_), channel_id=1, source_target_pairs={{0,8},{8,0},{16,24},{24,16},{1,9},{9,1},{17,25},{25,17},{2,10},{10... | collective-permute-start | bytes 995336 | tf_op jit(solution)/shard_map/ppermute | solution.py:254
  217.9 10.2 %collective-permute-start.49 = (f32[648,128]{1,0:T(8,128)S(1)}, f32[648,128]{1,0:T(8,128)S(1)}, u32[]{:S(2)}, u32[]{:S(2)}) collective-permute-start(f32[648,128]{1,0:T(8,128)S(1)} %get-tuple-element.347), channel_id=1, source_target_pairs={{0,4},{4,0},{1,5},{5,1},{2,6},{6,2},{3,7},{7,3},{8,12},{12,8},{9,1... | collective-permute-start | bytes 995336 | tf_op jit(solution)/shard_map/ppermute | solution.py:254
  219.2 8.9 %collective-permute-start.50 = (f32[648,128]{1,0:T(8,128)S(1)}, f32[648,128]{1,0:T(8,128)S(1)}, u32[]{:S(2)}, u32[]{:S(2)}) collective-permute-start(f32[648,128]{1,0:T(8,128)S(1)} %get-tuple-element.348), channel_id=1, source_target_pairs={{0,8},{8,0},{16,24},{24,16},{1,9},{9,1},{17,25},{25,17},{2,10},{10... | collective-permute-start | bytes 995336 | tf_op jit(solution)/shard_map/ppermute | solution.py:254
  228.2 10.3 %collective-permute-start.52 = (f32[648,128]{1,0:T(8,128)S(1)}, f32[648,128]{1,0:T(8,128)S(1)}, u32[]{:S(2)}, u32[]{:S(2)}) collective-permute-start(f32[648,128]{1,0:T(8,128)S(1)} %add.207), channel_id=1, source_target_pairs={{0,8},{8,0},{16,24},{24,16},{1,9},{9,1},{17,25},{25,17},{2,10},{10... | collective-permute-start | bytes 995336 | tf_op jit(solution)/shard_map/ppermute | solution.py:254
  229.9 9.9 %collective-permute-start.51 = (f32[648,128]{1,0:T(8,128)S(1)}, f32[648,128]{1,0:T(8,128)S(1)}, u32[]{:S(2)}, u32[]{:S(2)}) collective-permute-start(f32[648,128]{1,0:T(8,128)S(1)} %get-tuple-element.358), channel_id=1, source_target_pairs={{0,4},{4,0},{1,5},{5,1},{2,6},{6,2},{3,7},{7,3},{8,12},{12,8},{9,1... | collective-permute-start | bytes 995336 | tf_op jit(solution)/shard_map/ppermute | solution.py:254
  230.7 9.7 %collective-permute-start.54 = (f32[648,128]{1,0:T(8,128)S(1)}, f32[648,128]{1,0:T(8,128)S(1)}, u32[]{:S(2)}, u32[]{:S(2)}) collective-permute-start(f32[648,128]{1,0:T(8,128)S(1)} %fusion.3), channel_id=1, source_target_pairs={{0,2},{2,0},{1,3},{3,1},{4,6},{6,4},{5,7},{7,5},{8,10},{10,8},{9,1... | collective-permute-start | bytes 995336 | tf_op jit(solution)/shard_map/ppermute | solution.py:254
  240.8 8.9 %collective-permute-start.58 = (f32[648,128]{1,0:T(8,128)S(1)}, f32[648,128]{1,0:T(8,128)S(1)}, u32[]{:S(2)}, u32[]{:S(2)}) collective-permute-start(f32[648,128]{1,0:T(8,128)S(1)} %get-tuple-element.376.refs_0_.refs_3_), channel_id=1, source_target_pairs={{0,2},{2,0},{1,3},{3,1},{4,6},{6,4},{5,7},{7,5},{8,10},{10,8},{9,1... | collective-permute-start | bytes 995336 | tf_op jit(solution)/shard_map/ppermute | solution.py:254
  243.1 11.5 %collective-permute-start.56 = (f32[648,128]{1,0:T(8,128)S(1)}, f32[648,128]{1,0:T(8,128)S(1)}, u32[]{:S(2)}, u32[]{:S(2)}) collective-permute-start(f32[648,128]{1,0:T(8,128)S(1)} %add.210), channel_id=1, source_target_pairs={{0,8},{8,0},{16,24},{24,16},{1,9},{9,1},{17,25},{25,17},{2,10},{10... | collective-permute-start | bytes 995336 | tf_op jit(solution)/shard_map/ppermute | solution.py:254
  254.6 13.7 %collective-permute-start.55 = (f32[648,128]{1,0:T(8,128)S(1)}, f32[648,128]{1,0:T(8,128)S(1)}, u32[]{:S(2)}, u32[]{:S(2)}) collective-permute-start(f32[648,128]{1,0:T(8,128)S(1)} %add.209), channel_id=1, source_target_pairs={{0,4},{4,0},{1,5},{5,1},{2,6},{6,2},{3,7},{7,3},{8,12},{12,8},{9,1... | collective-permute-start | bytes 995336 | tf_op jit(solution)/shard_map/ppermute | solution.py:254
  255.4 13.0 %collective-permute-start.61 = (f32[648,128]{1,0:T(8,128)S(1)}, f32[648,128]{1,0:T(8,128)S(1)}, u32[]{:S(2)}, u32[]{:S(2)}) collective-permute-start(f32[648,128]{1,0:T(8,128)S(1)} %add.213), channel_id=1, source_target_pairs={{8,16},{16,8},{9,17},{17,9},{10,18},{18,10},{11,19},{19,11},{12,20... | collective-permute-start | bytes 995336 | tf_op jit(solution)/shard_map/ppermute | solution.py:268
  256.1 12.5 %collective-permute-start.60 = (f32[648,128]{1,0:T(8,128)S(1)}, f32[648,128]{1,0:T(8,128)S(1)}, u32[]{:S(2)}, u32[]{:S(2)}) collective-permute-start(f32[648,128]{1,0:T(8,128)S(1)} %add.212), channel_id=1, source_target_pairs={{0,8},{8,0},{16,24},{24,16},{1,9},{9,1},{17,25},{25,17},{2,10},{10... | collective-permute-start | bytes 995336 | tf_op jit(solution)/shard_map/ppermute | solution.py:254
  269.0 10.8 %collective-permute-start.63 = (f32[648,128]{1,0:T(8,128)S(1)}, f32[648,128]{1,0:T(8,128)S(1)}, u32[]{:S(2)}, u32[]{:S(2)}) collective-permute-start(f32[648,128]{1,0:T(8,128)S(1)} %get-tuple-element.394.refs_0_.refs_1_), channel_id=1, source_target_pairs={{0,8},{8,0},{16,24},{24,16},{1,9},{9,1},{17,25},{25,17},{2,10},{10... | collective-permute-start | bytes 995336 | tf_op jit(solution)/shard_map/ppermute | solution.py:254
  270.8 9.0 %collective-permute-start.64 = (f32[648,128]{1,0:T(8,128)S(1)}, f32[648,128]{1,0:T(8,128)S(1)}, u32[]{:S(2)}, u32[]{:S(2)}) collective-permute-start(f32[648,128]{1,0:T(8,128)S(1)} %get-tuple-element.394.refs_0_.refs_1_), channel_id=1, source_target_pairs={{8,16},{16,8},{9,17},{17,9},{10,18},{18,10},{11,19},{19,11},{12,20... | collective-permute-start | bytes 995336 | tf_op jit(solution)/shard_map/ppermute | solution.py:268
  271.5 10.8 %collective-permute-start.65 = (f32[648,128]{1,0:T(8,128)S(1)}, f32[648,128]{1,0:T(8,128)S(1)}, u32[]{:S(2)}, u32[]{:S(2)}) collective-permute-start(f32[648,128]{1,0:T(8,128)S(1)} %get-tuple-element.396), channel_id=1, source_target_pairs={{0,4},{4,0},{1,5},{5,1},{2,6},{6,2},{3,7},{7,3},{8,12},{12,8},{9,1... | collective-permute-start | bytes 995336 | tf_op jit(solution)/shard_map/ppermute | solution.py:254
  272.9 12.4 %collective-permute-start.66 = (f32[648,128]{1,0:T(8,128)S(1)}, f32[648,128]{1,0:T(8,128)S(1)}, u32[]{:S(2)}, u32[]{:S(2)}) collective-permute-start(f32[648,128]{1,0:T(8,128)S(1)} %get-tuple-element.397), channel_id=1, source_target_pairs={{0,8},{8,0},{16,24},{24,16},{1,9},{9,1},{17,25},{25,17},{2,10},{10... | collective-permute-start | bytes 995336 | tf_op jit(solution)/shard_map/ppermute | solution.py:254
  274.9 14.0 %collective-permute-start.69 = (f32[648,128]{1,0:T(8,128)S(1)}, f32[648,128]{1,0:T(8,128)S(1)}, u32[]{:S(2)}, u32[]{:S(2)}) collective-permute-start(f32[648,128]{1,0:T(8,128)S(1)} %get-tuple-element.394.refs_0_.refs_1_), channel_id=1, source_target_pairs={{0,4},{4,0},{1,5},{5,1},{2,6},{6,2},{3,7},{7,3},{8,12},{12,8},{9,1... | collective-permute-start | bytes 995336 | tf_op jit(solution)/shard_map/ppermute | solution.py:254
  285.4 8.3 %collective-permute-start.67 = (f32[648,128]{1,0:T(8,128)S(1)}, f32[648,128]{1,0:T(8,128)S(1)}, u32[]{:S(2)}, u32[]{:S(2)}) collective-permute-start(f32[648,128]{1,0:T(8,128)S(1)} %get-tuple-element.464), channel_id=1, source_target_pairs={{0,8},{8,0},{16,24},{24,16},{1,9},{9,1},{17,25},{25,17},{2,10},{10... | collective-permute-start | bytes 995336 | tf_op jit(solution)/shard_map/ppermute | solution.py:254
  295.2 8.5 %collective-permute-start.73 = (f32[648,128]{1,0:T(8,128)S(1)}, f32[648,128]{1,0:T(8,128)S(1)}, u32[]{:S(2)}, u32[]{:S(2)}) collective-permute-start(f32[648,128]{1,0:T(8,128)S(1)} %add.216), channel_id=1, source_target_pairs={{8,16},{16,8},{9,17},{17,9},{10,18},{18,10},{11,19},{19,11},{12,20... | collective-permute-start | bytes 995336 | tf_op jit(solution)/shard_map/ppermute | solution.py:268
  296.2 10.3 %collective-permute-start.72 = (f32[648,128]{1,0:T(8,128)S(1)}, f32[648,128]{1,0:T(8,128)S(1)}, u32[]{:S(2)}, u32[]{:S(2)}) collective-permute-start(f32[648,128]{1,0:T(8,128)S(1)} %get-tuple-element.462), channel_id=1, source_target_pairs={{0,8},{8,0},{16,24},{24,16},{1,9},{9,1},{17,25},{25,17},{2,10},{10... | collective-permute-start | bytes 995336 | tf_op jit(solution)/shard_map/ppermute | solution.py:254
  301.5 10.8 %collective-permute-start.71 = (f32[648,128]{1,0:T(8,128)S(1)}, f32[648,128]{1,0:T(8,128)S(1)}, u32[]{:S(2)}, u32[]{:S(2)}) collective-permute-start(f32[648,128]{1,0:T(8,128)S(1)} %broadcast_select_fusion.4.refs_2_), channel_id=1, source_target_pairs={{0,4},{4,0},{1,5},{5,1},{2,6},{6,2},{3,7},{7,3},{8,12},{12,8},{9,1... | collective-permute-start | bytes 995336 | tf_op jit(solution)/shard_map/ppermute | solution.py:254
  302.9 15.4 %collective-permute-start.76 = (f32[648,128]{1,0:T(8,128)S(1)}, f32[648,128]{1,0:T(8,128)S(1)}, u32[]{:S(2)}, u32[]{:S(2)}) collective-permute-start(f32[648,128]{1,0:T(8,128)S(1)} %add.217), channel_id=1, source_target_pairs={{0,4},{4,0},{1,5},{5,1},{2,6},{6,2},{3,7},{7,3},{8,12},{12,8},{9,1... | collective-permute-start | bytes 995336 | tf_op jit(solution)/shard_map/ppermute | solution.py:254
  316.3 10.7 %collective-permute-start.75 = (f32[648,128]{1,0:T(8,128)S(1)}, f32[648,128]{1,0:T(8,128)S(1)}, u32[]{:S(2)}, u32[]{:S(2)}) collective-permute-start(f32[648,128]{1,0:T(8,128)S(1)} %collective-permute-done.69.refs_4_), channel_id=1, source_target_pairs={{0,8},{8,0},{16,24},{24,16},{1,9},{9,1},{17,25},{25,17},{2,10},{10... | collective-permute-start | bytes 995336 | tf_op jit(solution)/shard_map/ppermute | solution.py:254
  327.4 10.0 %collective-permute-start.79 = (f32[648,128]{1,0:T(8,128)S(1)}, f32[648,128]{1,0:T(8,128)S(1)}, u32[]{:S(2)}, u32[]{:S(2)}) collective-permute-start(f32[648,128]{1,0:T(8,128)S(1)} %get-tuple-element.436.refs_0_.refs_7_), channel_id=1, source_target_pairs={{0,8},{8,0},{16,24},{24,16},{1,9},{9,1},{17,25},{25,17},{2,10},{10... | collective-permute-start | bytes 995336 | tf_op jit(solution)/shard_map/ppermute | solution.py:254
  337.5 10.2 %collective-permute-start.85 = (f32[648,128]{1,0:T(8,128)S(1)}, f32[648,128]{1,0:T(8,128)S(1)}, u32[]{:S(2)}, u32[]{:S(2)}) collective-permute-start(f32[648,128]{1,0:T(8,128)S(1)} %get-tuple-element.436.refs_0_.refs_7_), channel_id=1, source_target_pairs={{0,4},{4,0},{1,5},{5,1},{2,6},{6,2},{3,7},{7,3},{8,12},{12,8},{9,1... | collective-permute-start | bytes 995336 | tf_op jit(solution)/shard_map/ppermute | solution.py:254
  338.9 10.9 %collective-permute-start.83 = (f32[648,128]{1,0:T(8,128)S(1)}, f32[648,128]{1,0:T(8,128)S(1)}, u32[]{:S(2)}, u32[]{:S(2)}) collective-permute-start(f32[648,128]{1,0:T(8,128)S(1)} %collective-permute-done.80), channel_id=1, source_target_pairs={{0,8},{8,0},{16,24},{24,16},{1,9},{9,1},{17,25},{25,17},{2,10},{10... | collective-permute-start | bytes 995336 | tf_op jit(solution)/shard_map/ppermute | solution.py:254
  342.5 9.7 %collective-permute-start.82 = (f32[648,128]{1,0:T(8,128)S(1)}, f32[648,128]{1,0:T(8,128)S(1)}, u32[]{:S(2)}, u32[]{:S(2)}) collective-permute-start(f32[648,128]{1,0:T(8,128)S(1)} %fusion.2), channel_id=1, source_target_pairs={{0,2},{2,0},{1,3},{3,1},{4,6},{6,4},{5,7},{7,5},{8,10},{10,8},{9,1... | collective-permute-start | bytes 995336 | tf_op jit(solution)/shard_map/ppermute | solution.py:254
  352.2 8.8 %collective-permute-start.86 = (f32[648,128]{1,0:T(8,128)S(1)}, f32[648,128]{1,0:T(8,128)S(1)}, u32[]{:S(2)}, u32[]{:S(2)}) collective-permute-start(f32[648,128]{1,0:T(8,128)S(1)} %broadcast_select_fusion.1.refs_2_), channel_id=1, source_target_pairs={{0,4},{4,0},{1,5},{5,1},{2,6},{6,2},{3,7},{7,3},{8,12},{12,8},{9,1... | collective-permute-start | bytes 995336 | tf_op jit(solution)/shard_map/ppermute | solution.py:254
  352.9 8.4 %collective-permute-start.87 = (f32[648,128]{1,0:T(8,128)S(1)}, f32[648,128]{1,0:T(8,128)S(1)}, u32[]{:S(2)}, u32[]{:S(2)}) collective-permute-start(f32[648,128]{1,0:T(8,128)S(1)} %collective-permute-done.84), channel_id=1, source_target_pairs={{0,8},{8,0},{16,24},{24,16},{1,9},{9,1},{17,25},{25,17},{2,10},{10... | collective-permute-start | bytes 995336 | tf_op jit(solution)/shard_map/ppermute | solution.py:254
  379.4 9.9 %collective-permute-start.91 = (f32[648,128]{1,0:T(8,128)S(1)}, f32[648,128]{1,0:T(8,128)S(1)}, u32[]{:S(2)}, u32[]{:S(2)}) collective-permute-start(f32[648,128]{1,0:T(8,128)S(1)} %fusion.1), channel_id=1, source_target_pairs={{0,2},{2,0},{1,3},{3,1},{4,6},{6,4},{5,7},{7,5},{8,10},{10,8},{9,1... | collective-permute-start | bytes 995336 | tf_op jit(solution)/shard_map/ppermute | solution.py:254
  (35 other events, 206.9 us)
where the time goes:
time: 416 us; the launch traced here: 409 us
  waiting for transfers between devices  179 us (43%)
  starting transfers between devices  121 us (29%)
  Pallas kernels  66.5 us (16%)
  blocking collectives  28.7 us (7%)
  local copies, waits for them, and re-layouts  6.09 us (1%)
  other arithmetic  5.75 us (1%)
    ppermute x81, waiting for transfers between devices, swap(): return lax.ppermute(values, axis, [(i, i ^ k) for i in range(size)])  179 us
    ppermute x81, starting transfers between devices, swap(): return lax.ppermute(values, axis, [(i, i ^ k) for i in range(size)])  109 us
    pallas_call x8, Pallas kernels, product(): pl.pallas_call(functools.partial(product_kernel, adjoint, places, outs),...  59.8 us
    all_to_all x1, blocking collectives, exchange(): packed = lax.all_to_all(packed, REC, 0, 0, tiled=True)  28.7 us
    ppermute x16, starting transfers between devices, lax.ppermute(values, 'z', [(1, 2), (2, 1)])  12.2 us
  transfers between devices with their start and end apart: 97, of which 57 were waited for; matrix products, arithmetic and copies ran while one was open for 1% of the time, Pallas kernels for 13%

commit v1 on v0

--- a/solution.py
+++ b/solution.py
@@ -30,13 +30,13 @@
     return dot(left[0], right[0]) + (dot(left[0], right[1]) + dot(left[1], right[0]))
 
 
-def dot_exact(chosen, values):
+def dot_exact(chosen, values, dims):
     total = None
     for _ in range(3):
         part = values.astype(jnp.bfloat16)
         values = values - part.astype(jnp.float32)
         term = lax.dot_general(
-            chosen, part, (((0,), (0,)), ((), ())), preferred_element_type=jnp.float32
+            chosen, part, (dims, ((), ())), preferred_element_type=jnp.float32
         )
         total = term if total is None else total + term
     return total
@@ -109,7 +109,7 @@
         steps, shape, given, made = columns // tile, (2, 1, rows, tile), rows, columns
         k_spec = pl.BlockSpec(shape, lambda i: (0, slab, 0, i))
     else:
-        tile = rows // 2
+        tile = rows // 4
         steps, shape, given, made = rows // tile, (2, 1, tile, columns), columns, rows
         k_spec = pl.BlockSpec(shape, lambda i: (0, slab, i, 0))
     shapes = [
@@ -167,34 +167,58 @@
 
 
 def pack_kernel(slab, place_ref, mark_ref, traces_ref, packed_ref):
-    slots, width = packed_ref.shape[0], 2 * SOURCES
+    marked = len(packed_ref.shape) == 3
+    width = 2 * SOURCES
+    if marked:
+        peer = (packed_ref.shape[1] - HEAD) // CHUNKS
+        slots = packed_ref.shape[0] * peer
+    else:
+        slots = packed_ref.shape[0]
     spots = lax.broadcasted_iota(jnp.int32, (place_ref.shape[0], slots), 1)
     chosen = (place_ref[...] == spots).astype(jnp.bfloat16)
+    if marked:
+        marks = jnp.broadcast_to(mark_ref[...], (HEAD, mark_ref.shape[1])).astype(jnp.bfloat16)
+        marks = jnp.dot(marks, chosen, preferred_element_type=jnp.float32)
+        packed_ref[:, :HEAD, :] = jnp.zeros((packed_ref.shape[0], HEAD, LANES), jnp.float32)
+        for area in range(packed_ref.shape[0]):
+            packed_ref[area, :HEAD, :peer] = marks[:, area * peer : (area + 1) * peer]
     for part in range(2):
-        start = (part * FREQS + slab) * SOURCES
-        packed_ref[:, part * SOURCES : (part + 1) * SOURCES] = dot_exact(
-            chosen, traces_ref[:, start : start + SOURCES]
-        )
-    if packed_ref.shape[1] > width:
-        marks = jnp.broadcast_to(mark_ref[...], (mark_ref.shape[0], LANES))
-        packed_ref[:, width:] = dot_exact(chosen, marks)
-
-
-def unpack_kernel(sources, *refs):
-    mark_ref, part_refs, (piece_ref, marks, data) = refs[0], refs[1:-3], refs[-3:]
-    slots, width = data.shape
+        column = (part * FREQS + slab) * SOURCES
+        packed = dot_exact(chosen, traces_ref[:, column : column + SOURCES], ((0,), (0,)))
+        if not marked:
+            packed_ref[:, part * SOURCES : (part + 1) * SOURCES] = packed
+            continue
+        for chunk in range(CHUNKS // 2):
+            start = HEAD + (part * CHUNKS // 2 + chunk) * peer
+            lanes = slice(chunk * LANES, (chunk + 1) * LANES)
+            for area in range(packed_ref.shape[0]):
+                packed_ref[area, start : start + peer, :] = packed[
+                    area * peer : (area + 1) * peer, lanes
+                ]
+
+
+def unpack_kernel(sources, peer, mark_ref, *refs):
+    part_refs, (piece_ref, marks, data) = refs[:-3], refs[-3:]
+    slots = data.shape[0]
     rows = (piece_ref.shape[0] - HEAD) // CHUNKS
-    if sources is None:
-        marks[...], data[...] = mark_ref[:, :1], part_refs[0][:, :width]
-    else:
-        peer = slots // len(sources)
-        for index, (part, start, source) in enumerate(sources):
-            here = slice(index * peer, (index + 1) * peer)
-            marks[here, :] = mark_ref[pl.ds(pl.multiple_of(source() * peer, peer), peer), :1]
+    for index in range(slots // peer):
+        here = slice(index * peer, (index + 1) * peer)
+        if sources is None:
+            marks[:, here] = mark_ref[index, :HEAD, :peer]
+            if part_refs:
+                data[here, :] = part_refs[0][here, :]
+                continue
+            for chunk in range(CHUNKS):
+                start = HEAD + chunk * peer
+                lanes = slice(chunk * LANES, (chunk + 1) * LANES)
+                data[here, lanes] = mark_ref[index, start : start + peer, :]
+        else:
+            part, start, source = sources[index]
+            marks[:, here] = mark_ref[source(), :HEAD, :peer]
             data[here, :] = part_refs[part][start * peer : (start + 1) * peer, :]
-    spots = lax.broadcasted_iota(jnp.int32, (slots, rows), 1) + 1
-    chosen = (marks[...].astype(jnp.int32) == spots).astype(jnp.bfloat16)
-    placed = dot_exact(chosen, data[...])
+    spots = lax.broadcasted_iota(jnp.int32, (rows, slots), 0) + 1
+    chosen = (marks[:1, :].astype(jnp.int32) == spots).astype(jnp.bfloat16)
+    placed = dot_exact(chosen, data[...], ((1,), (0,)))
     for chunk in range(CHUNKS):
         start = HEAD + chunk * rows
         piece_ref[start : start + rows, :] = placed[:, chunk * LANES : (chunk + 1) * LANES]
@@ -212,40 +236,42 @@
         self.area = jnp.where(iota < counts[0, 0], ids // row_count, -1)
         before = (self.area[:, None] == self.area[None, :]) & (iota[None, :] < iota[:, None])
         self.rank = jnp.sum(before.astype(jnp.int32), axis=1)
-        self.mark = (ids % row_count + 1).astype(jnp.float32)[:, None]
+        self.mark = (ids % row_count + 1).astype(jnp.float32)[None, :]
 
     def pack(self, slab, marked, order):
         place = jnp.where(self.area >= 0, order * self.peer + self.rank, -1)
-        width = 2 * SOURCES
-        slots = self.areas * self.peer
+        shape = (self.areas * self.peer, 2 * SOURCES)
+        if marked:
+            shape = (self.areas, HEAD + CHUNKS * self.peer, LANES)
         return pl.pallas_call(
             functools.partial(pack_kernel, slab),
-            out_shape=jax.ShapeDtypeStruct((slots, width + LANES * marked), jnp.float32),
+            out_shape=jax.ShapeDtypeStruct(shape, jnp.float32),
             compiler_params=pltpu.CompilerParams(vmem_limit_bytes=SMALL_VMEM_BYTES),
         )(place[:, None], self.mark, self.traces)
 
     def exchange(self, slab, marked):
-        packed = self.pack(slab, marked, self.area).reshape(self.areas, self.peer, -1)
-        packed = lax.all_to_all(packed, REC, 0, 0, tiled=True)
-        return packed.reshape(self.areas * self.peer, -1)
-
-    def unpack(self, marks, parts, sources=None):
+        packed = self.pack(slab, marked, self.area)
+        if marked:
+            return lax.all_to_all(packed, REC, 0, 0, tiled=True)
+        packed = packed.reshape(self.areas, self.peer, -1)
+        return lax.all_to_all(packed, REC, 0, 0, tiled=True).reshape(self.areas * self.peer, -1)
+
+    def unpack(self, parts, sources=None):
         slots, width = self.areas * self.peer, 2 * SOURCES
         shape = (HEAD + CHUNKS * self.row_count, LANES)
         return pl.pallas_call(
-            functools.partial(unpack_kernel, sources),
+            functools.partial(unpack_kernel, sources, self.peer),
             out_shape=jax.ShapeDtypeStruct(shape, jnp.float32),
             scratch_shapes=[
-                pltpu.VMEM((slots, 1), jnp.float32),
+                pltpu.VMEM((HEAD, slots), jnp.float32),
                 pltpu.VMEM((slots, width), jnp.float32),
             ],
             compiler_params=pltpu.CompilerParams(vmem_limit_bytes=SMALL_VMEM_BYTES),
-        )(marks, *parts)
+        )(self.marks, *parts)
 
     def first(self):
-        received = self.exchange(0, True)
-        self.marks = received[:, 2 * SOURCES :]
-        self.piece = self.unpack(self.marks, [received])
+        self.marks = self.exchange(0, True)
+        self.piece = self.unpack([])
         return self.piece
 
 
@@ -315,7 +341,6 @@
 
 
 class Neighbours:
-    side = "z"
     rec_outs = [[rec_place(kind, across)] for across in (0, 1) for kind in KINDS]
     src_outs = [[src_place(0, 1), src_place(1, 1)], [src_place(1, 0)], [src_place(0, 0)]]
 
@@ -355,28 +380,37 @@
             for part, k in ((0, 0), (1, 3), (2, 2), (3, 1))
             for start in range(2)
         ]
-        return given.unpack(given.marks, [sent[0], *parts], sources)
-
-    def scatter_rec(self, blocks):
+        return given.unpack([sent[0], *parts], sources)
+
+    def scatter_rec(self, blocks, alone):
         blocks = yield tuple(("hold", block) for block in blocks)
         own, partner, third, far, own_y, partner_y, third_y, far_y = blocks
-        got_far, got_own_y, third_y, own_y, third = yield (
-            ("y", far_y), (self.side, partner_y), ("hold", third_y), ("hold", own_y), ("hold", third),
+        if alone:
+            got_far, third_y, third = yield ("y", far_y), ("hold", third_y), ("hold", third)
+            got_own_y = None
+        else:
+            got_far, got_own_y, third_y, third = yield (
+                ("y", far_y), ("z", partner_y), ("hold", third_y), ("hold", third),
+            )
+        far = far + got_far
+        got_third, got_far, third, far = yield (
+            ("y", third_y), ("up", far), ("hold", third), ("hold", far),
         )
-        far = far + got_far
-        got_third, got_far, got_own_y, own_y, third, far = yield (
-            ("y", third_y), ("up", far), ("hold", got_own_y), ("hold", own_y), ("hold", third),
-            ("hold", far),
-        )
-        own_y = own_y + got_own_y
         third = third + got_third
         far = far + got_far
-        got_own, got_third, got_partner, third = yield (
-            ("y~", own_y), ("up", third), ("mid", far), ("hold", third),
-        )
+        if alone:
+            got_y, got_third, got_partner, third = yield (
+                ("y", partner_y), ("up", third), ("mid", far), ("hold", third),
+            )
+            partner = partner + got_y
+        else:
+            own_y = own_y + got_own_y
+            got_third, got_partner, third, own_y = yield (
+                ("up", third), ("mid", far), ("hold", third), ("hold", own_y),
+            )
         partner = partner + got_partner
         third = third + got_third
-        last = yield ("hold", got_own), ("z", partner), ("mid", third)
+        last = yield ("y", own_y), ("z", partner), ("mid", third)
         return [own, *last]
 
     def scatter_src(self, blocks):
@@ -406,7 +440,7 @@
 
     def dispatch(self, given, slab, lag):
         (received,) = yield (("hold", given.exchange(slab, False)),)
-        return given.unpack(given.marks, [received])
+        return given.unpack([received])
 
     def gather_src(self, piece):
         (piece,) = yield (("hold", piece),)
@@ -416,7 +450,7 @@
         (piece,) = yield (("hold", piece),)
         return self.gather(piece, REC)
 
-    def scatter_rec(self, blocks):
+    def scatter_rec(self, blocks, alone):
         (blocks,) = yield (("hold", blocks),)
         return self.scatter(blocks, REC)
 
@@ -465,7 +499,7 @@
         pieces, places = yield from moves.gather_src(piece)
         rows = column_count if len(moves.rec_outs) > 1 else kernel.shape[3]
         blocks = product(kernel, slab, True, pieces, places, moves.rec_outs, rows)
-        return (yield from moves.scatter_rec(blocks))
+        return (yield from moves.scatter_rec(blocks, slab == 0))
 
     def forward(piece):
         pieces, places = yield from moves.gather_rec(piece)
@@ -489,8 +523,8 @@
 def put_slab(out, slab, piece):
     rows, each = out.shape[0], CHUNKS // 2
     for chunk in range(CHUNKS):
-        at = (chunk // each * FREQS + slab) * SOURCES + chunk % each * LANES
-        out[:, at : at + LANES] = piece[chunk * rows : (chunk + 1) * rows, :]
+        at = chunk % each * LANES
+        out[:, chunk // each, slab, at : at + LANES] = piece[chunk * rows : (chunk + 1) * rows, :]
 
 
 def join_left_kernel(*refs):
@@ -525,15 +559,14 @@
 
 def join(kernel, pieces):
     rows, width = (pieces[0].shape[0] - HEAD) // CHUNKS, 2 * FREQS * SOURCES
-    joined = pl.pallas_call(
+    return pl.pallas_call(
         kernel,
-        out_shape=jax.ShapeDtypeStruct((rows, width), jnp.float32),
+        out_shape=jax.ShapeDtypeStruct((rows, 2, FREQS, SOURCES), jnp.float32),
         compiler_params=pltpu.CompilerParams(vmem_limit_bytes=SMALL_VMEM_BYTES),
         cost_estimate=pl.CostEstimate(
             flops=rows * width * 4, bytes_accessed=8 * rows * width, transcendentals=0
         ),
     )(*pieces)
-    return joined.reshape(rows, 2, FREQS, SOURCES)
 
 
 def on_device(kernel, traces, acq_lists, counts):

time: 416 us -> 399 us (0.959); the launches traced: 409 us -> 398 us
  waiting for transfers between devices: 179 us -> 171 us
    ppermute x81, waiting for transfers between devices: 179 us -> 171 us  [swap(): return lax.ppermute(values, axis, [(i, i ^ k) for i in range(size)])]
  transfers between devices with their start and end apart: 97 -> 97, of which waited for: 57 -> 57; matrix products, arithmetic and copies ran while one was open for 1% -> 1% of each run, Pallas kernels for 13% -> 15%
where the time goes in v1:
time: 399 us; the launch traced here: 398 us
  waiting for transfers between devices  171 us (43%)
  starting transfers between devices  120 us (30%)
  Pallas kernels  70.4 us (18%)
  blocking collectives  25.4 us (6%)
  other arithmetic  5.6 us (1%)
    ppermute x81, waiting for transfers between devices, swap(): return lax.ppermute(values, axis, [(i, i ^ k) for i in range(size)])  171 us
    ppermute x81, starting transfers between devices, swap(): return lax.ppermute(values, axis, [(i, i ^ k) for i in range(size)])  108 us
    pallas_call x8, Pallas kernels, product(): pl.pallas_call(functools.partial(product_kernel, adjoint, places, outs),...  61.8 us
    all_to_all x1, blocking collectives, exchange(): return lax.all_to_all(packed, REC, 0, 0, tiled=True)  25.4 us
    ppermute x16, starting transfers between devices, lax.ppermute(values, 'z', [(1, 2), (2, 1)])  12 us
  transfers between devices with their start and end apart: 97, of which 57 were waited for; matrix products, arithmetic and copies ran while one was open for 1% of the time, Pallas kernels for 15%

profile of v1, /device:TPU:0, one launch (start us, length us, event | category | flops | bytes accessed | tf_op | source)
XLA Modules:
  0.0 398.2 jit_solution(15797572665649594348)
XLA Ops:
  3.0 2.3 reshape.212.traces_ref
  6.7 25.4 %all_to_all.5.mark_ref = f32[8,168,128]{2,1,0:T(8,128)S(1)} all-to-all(f32[8,168,128]{2,1,0:T(8,128)S(1)} %shard_map.59), channel_id=1, replica_groups=mesh['z'=4,'y'=2,'x'=2,'c'=2] {'z','y'}, dimensions={0} | all-to-all | bytes 1376256 | tf_op jit(solution)/shard_map/all_to_all | solution.py:255
  36.5 8.9 %collective-permute-done.2 = f32[160,512]{1,0:T(8,128)S(1)} collective-permute-done((f32[160,512]{1,0:T(8,128)S(1)}, f32[160,512]{1,0:T(8,128)S(1)}, u32[]{:S(2)}, u32[]{:S(2)}) %collective-permute-start.2) | collective-permute-done | bytes 327712 | tf_op jit(solution)/shard_map/ppermute | solution.py:280
  47.1 7.6 %shard_map.62 = (f32[648,128]{1,0:T(8,128)S(1)}, f32[648,128]{1,0:T(8,128)S(1)}, f32[648,128]{1,0:T(8,128)S(1)}, f32[648,128]{1,0:T(8,128)S(1)}, f32[648,128]{1,...) custom-call(f32[2,2,640,1280]{3,2,1,0:T(8,128)} %k_ref.15, ...), custom_call_target="tpu_custom_call" | custom-call | flops 5033164800 | bytes 10485760 | tf_op jit(solution)/shard_map/pallas_call | solution.py:118
  54.7 1.9 collective-permute-done.4.refs_3_
  59.3 8.5 %collective-permute-done.9.refs_2_ = f32[80,512]{1,0:T(8,128)S(1)} collective-permute-done((f32[80,512]{1,0:T(8,128)S(1)}, f32[80,512]{1,0:T(8,128)S(1)}, u32[]{:S(2)}, u32[]{:S(2)}) %collective-permute-start.9) | collective-permute-done | bytes 163872 | tf_op jit(solution)/shard_map/ppermute | solution.py:280
  71.3 6.2 %collective-permute-done.11 = f32[648,128]{1,0:T(8,128)S(1)} collective-permute-done((f32[648,128]{1,0:T(8,128)S(1)}, f32[648,128]{1,0:T(8,128)S(1)}, u32[]{:S(2)}, u32[]{:S(2)}) %collective-permute-start.11) | collective-permute-done | bytes 331808 | tf_op jit(solution)/shard_map/ppermute | solution.py:280
  79.4 4.7 %collective-permute-start.12 = (f32[648,128]{1,0:T(8,128)S(1)}, f32[648,128]{1,0:T(8,128)S(1)}, u32[]{:S(2)}, u32[]{:S(2)}) collective-permute-start(f32[648,128]{1,0:T(8,128)S(1)} %add.183), channel_id=1, source_target_pairs={{0,8},{8,0},{16,24},{24,16},{1,9},{9,1},{17,25},{25,17},{2,10},{10... | collective-permute-start | bytes 995336 | tf_op jit(solution)/shard_map/ppermute | solution.py:280
  84.8 4.7 %collective-permute-done.12 = f32[648,128]{1,0:T(8,128)S(1)} collective-permute-done((f32[648,128]{1,0:T(8,128)S(1)}, f32[648,128]{1,0:T(8,128)S(1)}, u32[]{:S(2)}, u32[]{:S(2)}) %collective-permute-start.12) | collective-permute-done | bytes 331808 | tf_op jit(solution)/shard_map/ppermute | solution.py:280
  91.0 3.5 collective-permute-start.16
  94.5 8.4 %shard_map.64 = (f32[648,128]{1,0:T(8,128)S(1)}, f32[648,128]{1,0:T(8,128)S(1)}, f32[648,128]{1,0:T(8,128)S(1)}, f32[648,128]{1,0:T(8,128)S(1)}, f32[648,128]{1,...) custom-call(f32[2,2,640,1280]{3,2,1,0:T(8,128)} %k_ref.15, ...), custom_call_target="tpu_custom_call" | custom-call | flops 5033164800 | bytes 10485760 | tf_op jit(solution)/shard_map/pallas_call | solution.py:118
  107.4 3.3 collective-permute-start.22
  111.6 2.8 collective-permute-done.19.refs_1_
  114.4 2.6 collective-permute-done.21
  117.0 3.2 collective-permute-done.22
  124.0 5.8 %collective-permute-done.23 = f32[648,128]{1,0:T(8,128)S(1)} collective-permute-done((f32[648,128]{1,0:T(8,128)S(1)}, f32[648,128]{1,0:T(8,128)S(1)}, u32[]{:S(2)}, u32[]{:S(2)}) %collective-permute-start.23) | collective-permute-done | bytes 331808 | tf_op jit(solution)/shard_map/ppermute | solution.py:280
  131.9 5.5 %collective-permute-start.28 = (f32[648,128]{1,0:T(8,128)S(1)}, f32[648,128]{1,0:T(8,128)S(1)}, u32[]{:S(2)}, u32[]{:S(2)}) collective-permute-start(f32[648,128]{1,0:T(8,128)S(1)} %get-tuple-element.446), channel_id=1, source_target_pairs={{0,8},{8,0},{16,24},{24,16},{1,9},{9,1},{17,25},{25,17},{2,10},{10... | collective-permute-start | bytes 995336 | tf_op jit(solution)/shard_map/ppermute | solution.py:280
  140.0 2.5 collective-permute-done.28
  142.5 2.1 collective-permute-done.27.refs_6_
  145.4 4.0 collective-permute-start.33
  151.5 5.2 %collective-permute-done.33.refs_2_ = f32[648,128]{1,0:T(8,128)S(1)} collective-permute-done((f32[648,128]{1,0:T(8,128)S(1)}, f32[648,128]{1,0:T(8,128)S(1)}, u32[]{:S(2)}, u32[]{:S(2)}) %collective-permute-start.33) | collective-permute-done | bytes 331808 | tf_op jit(solution)/shard_map/ppermute | solution.py:280
  158.3 3.1 collective-permute-done.31.refs_5_
  162.2 2.1 collective-permute-start.35
  165.0 7.6 %shard_map.66 = (f32[2,648,128]{2,1,0:T(8,128)S(1)}, f32[648,128]{1,0:T(8,128)S(1)}, f32[648,128]{1,0:T(8,128)S(1)}) custom-call(f32[2,2,640,1280]{3,2,1,0:T(8,128)} %k_ref.15, f32[648,128]{1,0:T(8,128)S(1)} %get-tuple-element.268.refs_0_.refs_4_, f32[648,128]{1,0:T(8,128)S(1)} %collective-permute-done.19.refs_1_, ...), custom_call_target="tpu_custom_call" | custom-call | flops 5033164800 | bytes 10485760 | tf_op jit(solution)/shard_map/pallas_call | solution.py:118
  177.2 5.7 %collective-permute-done.41.refs_4_ = f32[648,128]{1,0:T(8,128)S(1)} collective-permute-done((f32[648,128]{1,0:T(8,128)S(1)}, f32[648,128]{1,0:T(8,128)S(1)}, u32[]{:S(2)}, u32[]{:S(2)}) %collective-permute-start.41) | collective-permute-done | bytes 331808 | tf_op jit(solution)/shard_map/ppermute | solution.py:280
  184.0 2.3 collective-permute-done.38.refs_2_
  188.0 2.8 collective-permute-start.45
  190.8 4.3 %collective-permute-done.44.refs_6_ = f32[648,128]{1,0:T(8,128)S(1)} collective-permute-done((f32[648,128]{1,0:T(8,128)S(1)}, f32[648,128]{1,0:T(8,128)S(1)}, u32[]{:S(2)}, u32[]{:S(2)}) %collective-permute-start.44) | collective-permute-done | bytes 331808 | tf_op jit(solution)/shard_map/ppermute | solution.py:280
  195.9 3.4 collective-permute-done.45
  202.4 7.6 %shard_map.69 = (f32[648,128]{1,0:T(8,128)S(1)}, f32[648,128]{1,0:T(8,128)S(1)}, f32[648,128]{1,0:T(8,128)S(1)}, f32[648,128]{1,0:T(8,128)S(1)}, f32[648,128]{1,...) custom-call(f32[2,2,640,1280]{3,2,1,0:T(8,128)} %k_ref.15, ...), custom_call_target="tpu_custom_call" | custom-call | flops 5033164800 | bytes 10485760 | tf_op jit(solution)/shard_map/pallas_call | solution.py:118
  211.3 7.6 %shard_map.70 = (f32[2,648,128]{2,1,0:T(8,128)S(1)}, f32[648,128]{1,0:T(8,128)S(1)}, f32[648,128]{1,0:T(8,128)S(1)}) custom-call(f32[2,2,640,1280]{3,2,1,0:T(8,128)} %k_ref.15, f32[648,128]{1,0:T(8,128)S(1)} %get-tuple-element.306.refs_0_.refs_4_.refs_6_, f32[648,128]{1,0:T(8,128)S(1)} %collective-permute-done.35.refs_1_, ...), custom_call_target="tpu_custom_call" | custom-call | flops 5033164800 | bytes 10485760 | tf_op jit(solution)/shard_map/pallas_call | solution.py:118
  225.2 4.8 %collective-permute-done.53 = f32[648,128]{1,0:T(8,128)S(1)} collective-permute-done((f32[648,128]{1,0:T(8,128)S(1)}, f32[648,128]{1,0:T(8,128)S(1)}, u32[]{:S(2)}, u32[]{:S(2)}) %collective-permute-start.53) | collective-permute-done | bytes 331808 | tf_op jit(solution)/shard_map/ppermute | solution.py:280
  230.1 2.1 collective-permute-done.52
  234.9 3.2 collective-permute-start.56
  238.6 2.8 collective-permute-done.58.refs_1_
  241.4 4.9 %collective-permute-done.56 = f32[648,128]{1,0:T(8,128)S(1)} collective-permute-done((f32[648,128]{1,0:T(8,128)S(1)}, f32[648,128]{1,0:T(8,128)S(1)}, u32[]{:S(2)}, u32[]{:S(2)}) %collective-permute-start.56) | collective-permute-done | bytes 331808 | tf_op jit(solution)/shard_map/ppermute | solution.py:280
  248.0 4.6 %collective-permute-start.60 = (f32[648,128]{1,0:T(8,128)S(1)}, f32[648,128]{1,0:T(8,128)S(1)}, u32[]{:S(2)}, u32[]{:S(2)}) collective-permute-start(f32[648,128]{1,0:T(8,128)S(1)} %add_add_fusion), channel_id=1, source_target_pairs={{0,8},{8,0},{16,24},{24,16},{1,9},{9,1},{17,25},{25,17},{2,10},{10... | collective-permute-start | bytes 995336 | tf_op jit(solution)/shard_map/ppermute | solution.py:280
  252.6 7.6 %shard_map.72 = (f32[648,128]{1,0:T(8,128)S(1)}, f32[648,128]{1,0:T(8,128)S(1)}, f32[648,128]{1,0:T(8,128)S(1)}, f32[648,128]{1,0:T(8,128)S(1)}, f32[648,128]{1,...) custom-call(f32[2,2,640,1280]{3,2,1,0:T(8,128)} %k_ref.15, ...), custom_call_target="tpu_custom_call" | custom-call | flops 5033164800 | bytes 10485760 | tf_op jit(solution)/shard_map/pallas_call | solution.py:118
  264.7 2.1 collective-permute-start.66
  267.5 4.2 %collective-permute-done.63.refs_1_ = f32[648,128]{1,0:T(8,128)S(1)} collective-permute-done((f32[648,128]{1,0:T(8,128)S(1)}, f32[648,128]{1,0:T(8,128)S(1)}, u32[]{:S(2)}, u32[]{:S(2)}) %collective-permute-start.63) | collective-permute-done | bytes 331808 | tf_op jit(solution)/shard_map/ppermute | solution.py:280
  271.7 2.5 collective-permute-done.65
  274.2 3.0 collective-permute-done.66
  280.7 4.8 %collective-permute-done.67 = f32[648,128]{1,0:T(8,128)S(1)} collective-permute-done((f32[648,128]{1,0:T(8,128)S(1)}, f32[648,128]{1,0:T(8,128)S(1)}, u32[]{:S(2)}, u32[]{:S(2)}) %collective-permute-start.67) | collective-permute-done | bytes 331808 | tf_op jit(solution)/shard_map/ppermute | solution.py:280
  287.9 5.2 %collective-permute-start.72 = (f32[648,128]{1,0:T(8,128)S(1)}, f32[648,128]{1,0:T(8,128)S(1)}, u32[]{:S(2)}, u32[]{:S(2)}) collective-permute-start(f32[648,128]{1,0:T(8,128)S(1)} %get-tuple-element.442), channel_id=1, source_target_pairs={{0,8},{8,0},{16,24},{24,16},{1,9},{9,1},{17,25},{25,17},{2,10},{10... | collective-permute-start | bytes 995336 | tf_op jit(solution)/shard_map/ppermute | solution.py:280
  294.5 3.7 collective-permute-done.72
  298.2 2.1 collective-permute-done.71.refs_6_
  305.3 4.7 %collective-permute-done.77.refs_2_ = f32[648,128]{1,0:T(8,128)S(1)} collective-permute-done((f32[648,128]{1,0:T(8,128)S(1)}, f32[648,128]{1,0:T(8,128)S(1)}, u32[]{:S(2)}, u32[]{:S(2)}) %collective-permute-start.77) | collective-permute-done | bytes 331808 | tf_op jit(solution)/shard_map/ppermute | solution.py:280
  311.6 3.4 collective-permute-done.75.refs_5_
  315.6 2.4 collective-permute-start.79
  318.7 7.6 %shard_map.74 = (f32[2,648,128]{2,1,0:T(8,128)S(1)}, f32[648,128]{1,0:T(8,128)S(1)}, f32[648,128]{1,0:T(8,128)S(1)}) custom-call(f32[2,2,640,1280]{3,2,1,0:T(8,128)} %k_ref.15, f32[648,128]{1,0:T(8,128)S(1)} %get-tuple-element.376.refs_0_.refs_1_, f32[648,128]{1,0:T(8,128)S(1)} %collective-permute-done.63.refs_1_, ...), custom_call_target="tpu_custom_call" | custom-call | flops 5033164800 | bytes 10485760 | tf_op jit(solution)/shard_map/pallas_call | solution.py:118
  327.8 2.6 collective-permute-start.83
  332.0 4.6 %collective-permute-done.85.refs_4_ = f32[648,128]{1,0:T(8,128)S(1)} collective-permute-done((f32[648,128]{1,0:T(8,128)S(1)}, f32[648,128]{1,0:T(8,128)S(1)}, u32[]{:S(2)}, u32[]{:S(2)}) %collective-permute-start.85) | collective-permute-done | bytes 331808 | tf_op jit(solution)/shard_map/ppermute | solution.py:280
  336.6 1.9 collective-permute-done.83
  338.5 2.5 collective-permute-done.82.refs_2_
  341.9 1.8 collective-permute-start.87
  343.8 6.1 %collective-permute-done.86.refs_6_ = f32[648,128]{1,0:T(8,128)S(1)} collective-permute-done((f32[648,128]{1,0:T(8,128)S(1)}, f32[648,128]{1,0:T(8,128)S(1)}, u32[]{:S(2)}, u32[]{:S(2)}) %collective-permute-start.86) | collective-permute-done | bytes 331808 | tf_op jit(solution)/shard_map/ppermute | solution.py:280
  353.5 4.5 %collective-permute-done.88.refs_7_ = f32[648,128]{1,0:T(8,128)S(1)} collective-permute-done((f32[648,128]{1,0:T(8,128)S(1)}, f32[648,128]{1,0:T(8,128)S(1)}, u32[]{:S(2)}, u32[]{:S(2)}) %collective-permute-start.88) | collective-permute-done | bytes 331808 | tf_op jit(solution)/shard_map/ppermute | solution.py:280
  359.1 7.6 %shard_map.77 = (f32[2,648,128]{2,1,0:T(8,128)S(1)}, f32[648,128]{1,0:T(8,128)S(1)}, f32[648,128]{1,0:T(8,128)S(1)}) custom-call(f32[2,2,640,1280]{3,2,1,0:T(8,128)} %k_ref.15, f32[648,128]{1,0:T(8,128)S(1)} %get-tuple-element.416.refs_0_.refs_7_, f32[648,128]{1,0:T(8,128)S(1)} %collective-permute-done.79.refs_1_, ...), custom_call_target="tpu_custom_call" | custom-call | flops 5033164800 | bytes 10485760 | tf_op jit(solution)/shard_map/pallas_call | solution.py:118
  366.8 2.1 collective-permute-done.90
  370.0 8.9 %collective-permute-done.91.refs_2_ = f32[648,128]{1,0:T(8,128)S(1)} collective-permute-done((f32[648,128]{1,0:T(8,128)S(1)}, f32[648,128]{1,0:T(8,128)S(1)}, u32[]{:S(2)}, u32[]{:S(2)}) %collective-permute-start.91) | collective-permute-done | bytes 331808 | tf_op jit(solution)/shard_map/ppermute | solution.py:280
  381.0 3.1 collective-permute-done.93
  384.7 2.9 collective-permute-done.94
  389.3 2.0 collective-permute-done.95
  391.3 2.6 collective-permute-start.96
  (217 shorter events, 101.5 us)
Async XLA Ops:
  32.7 12.6 %collective-permute-start = (f32[648,128]{1,0:T(8,128)S(1)}, f32[648,128]{1,0:T(8,128)S(1)}, u32[]{:S(2)}, u32[]{:S(2)}) collective-permute-start(f32[648,128]{1,0:T(8,128)S(1)} %shard_map.60.refs_0_.refs_3_), channel_id=1, source_target_pairs={{0,2},{2,0},{1,3},{3,1},{4,6},{6,4},{5,7},{7,5},{8,10},{10,8},{9,1... | collective-permute-start | bytes 995336 | tf_op jit(solution)/shard_map/ppermute | solution.py:280
  34.3 11.1 %collective-permute-start.1 = (f32[648,128]{1,0:T(8,128)S(1)}, f32[648,128]{1,0:T(8,128)S(1)}, u32[]{:S(2)}, u32[]{:S(2)}) collective-permute-start(f32[648,128]{1,0:T(8,128)S(1)} %shard_map.60.refs_0_.refs_3_), channel_id=1, source_target_pairs={{0,1},{1,0},{2,3},{3,2},{4,5},{5,4},{6,7},{7,6},{8,9},{9,8},{10,11... | collective-permute-start | bytes 995336 | tf_op jit(solution)/shard_map/ppermute | solution.py:280
  35.1 10.2 %collective-permute-start.2 = (f32[160,512]{1,0:T(8,128)S(1)}, f32[160,512]{1,0:T(8,128)S(1)}, u32[]{:S(2)}, u32[]{:S(2)}) collective-permute-start(f32[160,512]{1,0:T(8,128)S(1)} %slice.57), channel_id=1, source_target_pairs={{0,4},{4,0},{1,5},{5,1},{2,6},{6,2},{3,7},{7,3},{8,12},{12,8},{9,1... | collective-permute-start | bytes 983048 | tf_op jit(solution)/shard_map/ppermute | solution.py:280
  45.4 9.3 %collective-permute-start.5 = (f32[80,512]{1,0:T(8,128)S(1)}, f32[80,512]{1,0:T(8,128)S(1)}, u32[]{:S(2)}, u32[]{:S(2)}) collective-permute-start(f32[80,512]{1,0:T(8,128)S(1)} %pad_maximum_fusion.1), channel_id=1, source_target_pairs={{0,24},{8,16},{16,8},{24,0},{1,25},{9,17},{17,9},{25,1},{2,26},{10... | collective-permute-start | bytes 491528 | tf_op jit(solution)/shard_map/ppermute | solution.py:280
  46.7 9.9 %collective-permute-start.4 = (f32[80,512]{1,0:T(8,128)S(1)}, f32[80,512]{1,0:T(8,128)S(1)}, u32[]{:S(2)}, u32[]{:S(2)}) collective-permute-start(f32[80,512]{1,0:T(8,128)S(1)} %pad_maximum_fusion), channel_id=1, source_target_pairs={{0,8},{8,0},{16,24},{24,16},{1,9},{9,1},{17,25},{25,17},{2,10},{10... | collective-permute-start | bytes 491528 | tf_op jit(solution)/shard_map/ppermute | solution.py:280
  56.6 11.2 %collective-permute-start.8 = (f32[648,128]{1,0:T(8,128)S(1)}, f32[648,128]{1,0:T(8,128)S(1)}, u32[]{:S(2)}, u32[]{:S(2)}) collective-permute-start(f32[648,128]{1,0:T(8,128)S(1)} %get-tuple-element.237), channel_id=1, source_target_pairs={{0,4},{4,0},{1,5},{5,1},{2,6},{6,2},{3,7},{7,3},{8,12},{12,8},{9,1... | collective-permute-start | bytes 995336 | tf_op jit(solution)/shard_map/ppermute | solution.py:280
  58.0 9.8 %collective-permute-start.9 = (f32[80,512]{1,0:T(8,128)S(1)}, f32[80,512]{1,0:T(8,128)S(1)}, u32[]{:S(2)}, u32[]{:S(2)}) collective-permute-start(f32[80,512]{1,0:T(8,128)S(1)} %pad_maximum_fusion.2), channel_id=1, source_target_pairs={{0,16},{8,24},{16,0},{24,8},{1,17},{9,25},{17,1},{25,9},{2,18},{10... | collective-permute-start | bytes 491528 | tf_op jit(solution)/shard_map/ppermute | solution.py:280
  67.8 9.7 %collective-permute-start.11 = (f32[648,128]{1,0:T(8,128)S(1)}, f32[648,128]{1,0:T(8,128)S(1)}, u32[]{:S(2)}, u32[]{:S(2)}) collective-permute-start(f32[648,128]{1,0:T(8,128)S(1)} %add.182), channel_id=1, source_target_pairs={{0,8},{8,0},{16,24},{24,16},{1,9},{9,1},{17,25},{25,17},{2,10},{10... | collective-permute-start | bytes 995336 | tf_op jit(solution)/shard_map/ppermute | solution.py:280
  67.9 10.7 %collective-permute-start.10 = (f32[648,128]{1,0:T(8,128)S(1)}, f32[648,128]{1,0:T(8,128)S(1)}, u32[]{:S(2)}, u32[]{:S(2)}) collective-permute-start(f32[648,128]{1,0:T(8,128)S(1)} %get-tuple-element.240), channel_id=1, source_target_pairs={{0,4},{4,0},{1,5},{5,1},{2,6},{6,2},{3,7},{7,3},{8,12},{12,8},{9,1... | collective-permute-start | bytes 995336 | tf_op jit(solution)/shard_map/ppermute | solution.py:280
  68.5 16.2 %collective-permute-start.7 = (f32[648,128]{1,0:T(8,128)S(1)}, f32[648,128]{1,0:T(8,128)S(1)}, u32[]{:S(2)}, u32[]{:S(2)}) collective-permute-start(f32[648,128]{1,0:T(8,128)S(1)} %get-tuple-element.236), channel_id=1, source_target_pairs={{0,4},{4,0},{1,5},{5,1},{2,6},{6,2},{3,7},{7,3},{8,12},{12,8},{9,1... | collective-permute-start | bytes 995336 | tf_op jit(solution)/shard_map/ppermute | solution.py:280
  70.7 14.0 %collective-permute-start.14 = (f32[648,128]{1,0:T(8,128)S(1)}, f32[648,128]{1,0:T(8,128)S(1)}, u32[]{:S(2)}, u32[]{:S(2)}) collective-permute-start(f32[648,128]{1,0:T(8,128)S(1)} %shard_map.63.refs_0_.refs_3_), channel_id=1, source_target_pairs={{0,2},{2,0},{1,3},{3,1},{4,6},{6,4},{5,7},{7,5},{8,10},{10,8},{9,1... | collective-permute-start | bytes 995336 | tf_op jit(solution)/shard_map/ppermute | solution.py:280
  71.3 13.4 %collective-permute-start.15 = (f32[648,128]{1,0:T(8,128)S(1)}, f32[648,128]{1,0:T(8,128)S(1)}, u32[]{:S(2)}, u32[]{:S(2)}) collective-permute-start(f32[648,128]{1,0:T(8,128)S(1)} %shard_map.63.refs_0_.refs_3_), channel_id=1, source_target_pairs={{0,1},{1,0},{2,3},{3,2},{4,5},{5,4},{6,7},{7,6},{8,9},{9,8},{10,11... | collective-permute-start | bytes 995336 | tf_op jit(solution)/shard_map/ppermute | solution.py:280
  79.4 10.0 %collective-permute-start.12 = (f32[648,128]{1,0:T(8,128)S(1)}, f32[648,128]{1,0:T(8,128)S(1)}, u32[]{:S(2)}, u32[]{:S(2)}) collective-permute-start(f32[648,128]{1,0:T(8,128)S(1)} %add.183), channel_id=1, source_target_pairs={{0,8},{8,0},{16,24},{24,16},{1,9},{9,1},{17,25},{25,17},{2,10},{10... | collective-permute-start | bytes 995336 | tf_op jit(solution)/shard_map/ppermute | solution.py:280
  89.4 13.5 %collective-permute-start.6 = (f32[648,128]{1,0:T(8,128)S(1)}, f32[648,128]{1,0:T(8,128)S(1)}, u32[]{:S(2)}, u32[]{:S(2)}) collective-permute-start(f32[648,128]{1,0:T(8,128)S(1)} %get-tuple-element.234), channel_id=1, source_target_pairs={{0,4},{4,0},{1,5},{5,1},{2,6},{6,2},{3,7},{7,3},{8,12},{12,8},{9,1... | collective-permute-start | bytes 995336 | tf_op jit(solution)/shard_map/ppermute | solution.py:280
  90.3 12.7 %collective-permute-start.17 = (f32[648,128]{1,0:T(8,128)S(1)}, f32[648,128]{1,0:T(8,128)S(1)}, u32[]{:S(2)}, u32[]{:S(2)}) collective-permute-start(f32[648,128]{1,0:T(8,128)S(1)} %add.187), channel_id=1, source_target_pairs={{8,16},{16,8},{9,17},{17,9},{10,18},{18,10},{11,19},{19,11},{12,20... | collective-permute-start | bytes 995336 | tf_op jit(solution)/shard_map/ppermute | solution.py:294
  91.0 11.9 %collective-permute-start.16 = (f32[648,128]{1,0:T(8,128)S(1)}, f32[648,128]{1,0:T(8,128)S(1)}, u32[]{:S(2)}, u32[]{:S(2)}) collective-permute-start(f32[648,128]{1,0:T(8,128)S(1)} %add_add_fusion.1), channel_id=1, source_target_pairs={{0,8},{8,0},{16,24},{24,16},{1,9},{9,1},{17,25},{25,17},{2,10},{10... | collective-permute-start | bytes 995336 | tf_op jit(solution)/shard_map/ppermute | solution.py:280
  103.7 10.7 %collective-permute-start.19 = (f32[648,128]{1,0:T(8,128)S(1)}, f32[648,128]{1,0:T(8,128)S(1)}, u32[]{:S(2)}, u32[]{:S(2)}) collective-permute-start(f32[648,128]{1,0:T(8,128)S(1)} %get-tuple-element.268.refs_0_.refs_4_), channel_id=1, source_target_pairs={{0,8},{8,0},{16,24},{24,16},{1,9},{9,1},{17,25},{25,17},{2,10},{10... | collective-permute-start | bytes 995336 | tf_op jit(solution)/shard_map/ppermute | solution.py:280
  104.6 9.8 %collective-permute-start.20 = (f32[648,128]{1,0:T(8,128)S(1)}, f32[648,128]{1,0:T(8,128)}, u32[]{:S(2)}, u32[]{:S(2)}) collective-permute-start(f32[648,128]{1,0:T(8,128)S(1)} %get-tuple-element.268.refs_0_.refs_4_), channel_id=1, source_target_pairs={{8,16},{16,8},{9,17},{17,9},{10,18},{18,10},{11,19},{19,11},{12,20... | collective-permute-start | bytes 995336 | tf_op jit(solution)/shard_map/ppermute | solution.py:294
  106.0 11.1 %collective-permute-start.21 = (f32[648,128]{1,0:T(8,128)}, f32[648,128]{1,0:T(8,128)}, u32[]{:S(2)}, u32[]{:S(2)}) collective-permute-start(f32[648,128]{1,0:T(8,128)} %get-tuple-element.269), channel_id=1, source_target_pairs={{0,4},{4,0},{1,5},{5,1},{2,6},{6,2},{3,7},{7,3},{8,12},{12,8},{9,1... | collective-permute-start | bytes 995336 | tf_op jit(solution)/shard_map/ppermute | solution.py:280
  107.4 12.8 %collective-permute-start.22 = (f32[648,128]{1,0:T(8,128)}, f32[648,128]{1,0:T(8,128)}, u32[]{:S(2)}, u32[]{:S(2)}) collective-permute-start(f32[648,128]{1,0:T(8,128)} %get-tuple-element.270), channel_id=1, source_target_pairs={{0,8},{8,0},{16,24},{24,16},{1,9},{9,1},{17,25},{25,17},{2,10},{10... | collective-permute-start | bytes 995336 | tf_op jit(solution)/shard_map/ppermute | solution.py:280
  110.8 13.2 %collective-permute-start.25 = (f32[648,128]{1,0:T(8,128)S(1)}, f32[648,128]{1,0:T(8,128)S(1)}, u32[]{:S(2)}, u32[]{:S(2)}) collective-permute-start(f32[648,128]{1,0:T(8,128)S(1)} %get-tuple-element.268.refs_0_.refs_4_), channel_id=1, source_target_pairs={{0,4},{4,0},{1,5},{5,1},{2,6},{6,2},{3,7},{7,3},{8,12},{12,8},{9,1... | collective-permute-start | bytes 995336 | tf_op jit(solution)/shard_map/ppermute | solution.py:280
  121.3 8.5 %collective-permute-start.23 = (f32[648,128]{1,0:T(8,128)S(1)}, f32[648,128]{1,0:T(8,128)S(1)}, u32[]{:S(2)}, u32[]{:S(2)}) collective-permute-start(f32[648,128]{1,0:T(8,128)S(1)} %get-tuple-element.448), channel_id=1, source_target_pairs={{0,8},{8,0},{16,24},{24,16},{1,9},{9,1},{17,25},{25,17},{2,10},{10... | collective-permute-start | bytes 995336 | tf_op jit(solution)/shard_map/ppermute | solution.py:280
  122.6 8.5 %collective-permute-start.26 = (f32[648,128]{1,0:T(8,128)S(1)}, f32[648,128]{1,0:T(8,128)S(1)}, u32[]{:S(2)}, u32[]{:S(2)}) collective-permute-start(f32[648,128]{1,0:T(8,128)S(1)} %copy-done.1), channel_id=1, source_target_pairs={{0,4},{4,0},{1,5},{5,1},{2,6},{6,2},{3,7},{7,3},{8,12},{12,8},{9,1... | collective-permute-start | bytes 995336 | tf_op jit(solution)/shard_map/ppermute | solution.py:280
  131.1 8.9 %collective-permute-start.29 = (f32[648,128]{1,0:T(8,128)S(1)}, f32[648,128]{1,0:T(8,128)S(1)}, u32[]{:S(2)}, u32[]{:S(2)}) collective-permute-start(f32[648,128]{1,0:T(8,128)S(1)} %add.190), channel_id=1, source_target_pairs={{8,16},{16,8},{9,17},{17,9},{10,18},{18,10},{11,19},{19,11},{12,20... | collective-permute-start | bytes 995336 | tf_op jit(solution)/shard_map/ppermute | solution.py:294
  131.9 10.6 %collective-permute-start.28 = (f32[648,128]{1,0:T(8,128)S(1)}, f32[648,128]{1,0:T(8,128)S(1)}, u32[]{:S(2)}, u32[]{:S(2)}) collective-permute-start(f32[648,128]{1,0:T(8,128)S(1)} %get-tuple-element.446), channel_id=1, source_target_pairs={{0,8},{8,0},{16,24},{24,16},{1,9},{9,1},{17,25},{25,17},{2,10},{10... | collective-permute-start | bytes 995336 | tf_op jit(solution)/shard_map/ppermute | solution.py:280
  145.4 11.4 %collective-permute-start.33 = (f32[648,128]{1,0:T(8,128)S(1)}, f32[648,128]{1,0:T(8,128)S(1)}, u32[]{:S(2)}, u32[]{:S(2)}) collective-permute-start(f32[648,128]{1,0:T(8,128)S(1)} %add.192), channel_id=1, source_target_pairs={{0,8},{8,0},{16,24},{24,16},{1,9},{9,1},{17,25},{25,17},{2,10},{10... | collective-permute-start | bytes 995336 | tf_op jit(solution)/shard_map/ppermute | solution.py:280
  149.4 8.9 %collective-permute-start.30 = (f32[648,128]{1,0:T(8,128)S(1)}, f32[648,128]{1,0:T(8,128)S(1)}, u32[]{:S(2)}, u32[]{:S(2)}) collective-permute-start(f32[648,128]{1,0:T(8,128)S(1)} %broadcast_select_fusion.8.refs_3_), channel_id=1, source_target_pairs={{0,4},{4,0},{1,5},{5,1},{2,6},{6,2},{3,7},{7,3},{8,12},{12,8},{9,1... | collective-permute-start | bytes 995336 | tf_op jit(solution)/shard_map/ppermute | solution.py:280
  150.7 10.7 %collective-permute-start.31 = (f32[648,128]{1,0:T(8,128)S(1)}, f32[648,128]{1,0:T(8,128)S(1)}, u32[]{:S(2)}, u32[]{:S(2)}) collective-permute-start(f32[648,128]{1,0:T(8,128)S(1)} %collective-permute-done.25.refs_4_), channel_id=1, source_target_pairs={{0,8},{8,0},{16,24},{24,16},{1,9},{9,1},{17,25},{25,17},{2,10},{10... | collective-permute-start | bytes 995336 | tf_op jit(solution)/shard_map/ppermute | solution.py:280
  150.7 11.1 %collective-permute-start.32 = (f32[648,128]{1,0:T(8,128)S(1)}, f32[648,128]{1,0:T(8,128)S(1)}, u32[]{:S(2)}, u32[]{:S(2)}) collective-permute-start(f32[648,128]{1,0:T(8,128)S(1)} %add.191), channel_id=1, source_target_pairs={{0,4},{4,0},{1,5},{5,1},{2,6},{6,2},{3,7},{7,3},{8,12},{12,8},{9,1... | collective-permute-start | bytes 995336 | tf_op jit(solution)/shard_map/ppermute | solution.py:280
  162.2 10.4 %collective-permute-start.35 = (f32[648,128]{1,0:T(8,128)S(1)}, f32[648,128]{1,0:T(8,128)S(1)}, u32[]{:S(2)}, u32[]{:S(2)}) collective-permute-start(f32[648,128]{1,0:T(8,128)S(1)} %get-tuple-element.306.refs_0_.refs_4_.refs_6_), channel_id=1, source_target_pairs={{0,8},{8,0},{16,24},{24,16},{1,9},{9,1},{17,25},{25,17},{2,10},{10... | collective-permute-start | bytes 995336 | tf_op jit(solution)/shard_map/ppermute | solution.py:280
  172.7 10.2 %collective-permute-start.41 = (f32[648,128]{1,0:T(8,128)S(1)}, f32[648,128]{1,0:T(8,128)S(1)}, u32[]{:S(2)}, u32[]{:S(2)}) collective-permute-start(f32[648,128]{1,0:T(8,128)S(1)} %get-tuple-element.306.refs_0_.refs_4_.refs_6_), channel_id=1, source_target_pairs={{0,4},{4,0},{1,5},{5,1},{2,6},{6,2},{3,7},{7,3},{8,12},{12,8},{9,1... | collective-permute-start | bytes 995336 | tf_op jit(solution)/shard_map/ppermute | solution.py:280
  174.0 9.9 %collective-permute-start.39 = (f32[648,128]{1,0:T(8,128)S(1)}, f32[648,128]{1,0:T(8,128)S(1)}, u32[]{:S(2)}, u32[]{:S(2)}) collective-permute-start(f32[648,128]{1,0:T(8,128)S(1)} %collective-permute-done.36), channel_id=1, source_target_pairs={{0,8},{8,0},{16,24},{24,16},{1,9},{9,1},{17,25},{25,17},{2,10},{10... | collective-permute-start | bytes 995336 | tf_op jit(solution)/shard_map/ppermute | solution.py:280
  176.6 9.7 %collective-permute-start.38 = (f32[648,128]{1,0:T(8,128)S(1)}, f32[648,128]{1,0:T(8,128)S(1)}, u32[]{:S(2)}, u32[]{:S(2)}) collective-permute-start(f32[648,128]{1,0:T(8,128)S(1)} %fusion.4), channel_id=1, source_target_pairs={{0,2},{2,0},{1,3},{3,1},{4,6},{6,4},{5,7},{7,5},{8,10},{10,8},{9,1... | collective-permute-start | bytes 995336 | tf_op jit(solution)/shard_map/ppermute | solution.py:280
  186.3 8.8 %collective-permute-start.44 = (f32[648,128]{1,0:T(8,128)S(1)}, f32[648,128]{1,0:T(8,128)S(1)}, u32[]{:S(2)}, u32[]{:S(2)}) collective-permute-start(f32[648,128]{1,0:T(8,128)S(1)} %broadcast_select_fusion.7.refs_2_), channel_id=1, source_target_pairs={{0,4},{4,0},{1,5},{5,1},{2,6},{6,2},{3,7},{7,3},{8,12},{12,8},{9,1... | collective-permute-start | bytes 995336 | tf_op jit(solution)/shard_map/ppermute | solution.py:280
  187.4 8.5 %collective-permute-start.42 = (f32[648,128]{1,0:T(8,128)S(1)}, f32[648,128]{1,0:T(8,128)S(1)}, u32[]{:S(2)}, u32[]{:S(2)}) collective-permute-start(f32[648,128]{1,0:T(8,128)S(1)} %get-tuple-element.314.refs_0_.refs_3_), channel_id=1, source_target_pairs={{0,2},{2,0},{1,3},{3,1},{4,6},{6,4},{5,7},{7,5},{8,10},{10,8},{9,1... | collective-permute-start | bytes 995336 | tf_op jit(solution)/shard_map/ppermute | solution.py:280
  188.0 11.3 %collective-permute-start.45 = (f32[648,128]{1,0:T(8,128)S(1)}, f32[648,128]{1,0:T(8,128)S(1)}, u32[]{:S(2)}, u32[]{:S(2)}) collective-permute-start(f32[648,128]{1,0:T(8,128)S(1)} %collective-permute-done.40), channel_id=1, source_target_pairs={{0,8},{8,0},{16,24},{24,16},{1,9},{9,1},{17,25},{25,17},{2,10},{10... | collective-permute-start | bytes 995336 | tf_op jit(solution)/shard_map/ppermute | solution.py:280
  199.3 10.7 %collective-permute-start.47 = (f32[648,128]{1,0:T(8,128)S(1)}, f32[648,128]{1,0:T(8,128)S(1)}, u32[]{:S(2)}, u32[]{:S(2)}) collective-permute-start(f32[648,128]{1,0:T(8,128)S(1)} %broadcast_select_fusion.6.refs_3_), channel_id=1, source_target_pairs={{0,4},{4,0},{1,5},{5,1},{2,6},{6,2},{3,7},{7,3},{8,12},{12,8},{9,1... | collective-permute-start | bytes 995336 | tf_op jit(solution)/shard_map/ppermute | solution.py:280
  200.6 9.9 %collective-permute-start.48 = (f32[648,128]{1,0:T(8,128)S(1)}, f32[648,128]{1,0:T(8,128)S(1)}, u32[]{:S(2)}, u32[]{:S(2)}) collective-permute-start(f32[648,128]{1,0:T(8,128)S(1)} %collective-permute-done.41.refs_4_), channel_id=1, source_target_pairs={{0,8},{8,0},{16,24},{24,16},{1,9},{9,1},{17,25},{25,17},{2,10},{10... | collective-permute-start | bytes 995336 | tf_op jit(solution)/shard_map/ppermute | solution.py:280
  210.5 9.2 %collective-permute-start.51 = (f32[648,128]{1,0:T(8,128)S(1)}, f32[648,128]{1,0:T(8,128)S(1)}, u32[]{:S(2)}, u32[]{:S(2)}) collective-permute-start(f32[648,128]{1,0:T(8,128)S(1)} %get-tuple-element.335), channel_id=1, source_target_pairs={{0,4},{4,0},{1,5},{5,1},{2,6},{6,2},{3,7},{7,3},{8,12},{12,8},{9,1... | collective-permute-start | bytes 995336 | tf_op jit(solution)/shard_map/ppermute | solution.py:280
  219.8 10.3 %collective-permute-start.53 = (f32[648,128]{1,0:T(8,128)S(1)}, f32[648,128]{1,0:T(8,128)S(1)}, u32[]{:S(2)}, u32[]{:S(2)}) collective-permute-start(f32[648,128]{1,0:T(8,128)S(1)} %add.195), channel_id=1, source_target_pairs={{0,8},{8,0},{16,24},{24,16},{1,9},{9,1},{17,25},{25,17},{2,10},{10... | collective-permute-start | bytes 995336 | tf_op jit(solution)/shard_map/ppermute | solution.py:280
  221.5 10.6 %collective-permute-start.52 = (f32[648,128]{1,0:T(8,128)S(1)}, f32[648,128]{1,0:T(8,128)S(1)}, u32[]{:S(2)}, u32[]{:S(2)}) collective-permute-start(f32[648,128]{1,0:T(8,128)S(1)} %get-tuple-element.344), channel_id=1, source_target_pairs={{0,4},{4,0},{1,5},{5,1},{2,6},{6,2},{3,7},{7,3},{8,12},{12,8},{9,1... | collective-permute-start | bytes 995336 | tf_op jit(solution)/shard_map/ppermute | solution.py:280
  222.4 9.8 %collective-permute-start.55 = (f32[648,128]{1,0:T(8,128)S(1)}, f32[648,128]{1,0:T(8,128)S(1)}, u32[]{:S(2)}, u32[]{:S(2)}) collective-permute-start(f32[648,128]{1,0:T(8,128)S(1)} %fusion.3), channel_id=1, source_target_pairs={{0,2},{2,0},{1,3},{3,1},{4,6},{6,4},{5,7},{7,5},{8,10},{10,8},{9,1... | collective-permute-start | bytes 995336 | tf_op jit(solution)/shard_map/ppermute | solution.py:280
  223.9 14.6 %collective-permute-start.50 = (f32[648,128]{1,0:T(8,128)S(1)}, f32[648,128]{1,0:T(8,128)S(1)}, u32[]{:S(2)}, u32[]{:S(2)}) collective-permute-start(f32[648,128]{1,0:T(8,128)S(1)} %get-tuple-element.334), channel_id=1, source_target_pairs={{0,4},{4,0},{1,5},{5,1},{2,6},{6,2},{3,7},{7,3},{8,12},{12,8},{9,1... | collective-permute-start | bytes 995336 | tf_op jit(solution)/shard_map/ppermute | solution.py:280
  232.6 8.8 %collective-permute-start.58 = (f32[648,128]{1,0:T(8,128)S(1)}, f32[648,128]{1,0:T(8,128)S(1)}, u32[]{:S(2)}, u32[]{:S(2)}) collective-permute-start(f32[648,128]{1,0:T(8,128)S(1)} %get-tuple-element.357.refs_0_.refs_3_), channel_id=1, source_target_pairs={{0,2},{2,0},{1,3},{3,1},{4,6},{6,4},{5,7},{7,5},{8,10},{10,8},{9,1... | collective-permute-start | bytes 995336 | tf_op jit(solution)/shard_map/ppermute | solution.py:280
  234.9 11.4 %collective-permute-start.56 = (f32[648,128]{1,0:T(8,128)S(1)}, f32[648,128]{1,0:T(8,128)S(1)}, u32[]{:S(2)}, u32[]{:S(2)}) collective-permute-start(f32[648,128]{1,0:T(8,128)S(1)} %add.197), channel_id=1, source_target_pairs={{0,8},{8,0},{16,24},{24,16},{1,9},{9,1},{17,25},{25,17},{2,10},{10... | collective-permute-start | bytes 995336 | tf_op jit(solution)/shard_map/ppermute | solution.py:280
  246.3 13.9 %collective-permute-start.49 = (f32[648,128]{1,0:T(8,128)S(1)}, f32[648,128]{1,0:T(8,128)S(1)}, u32[]{:S(2)}, u32[]{:S(2)}) collective-permute-start(f32[648,128]{1,0:T(8,128)S(1)} %get-tuple-element.332), channel_id=1, source_target_pairs={{0,4},{4,0},{1,5},{5,1},{2,6},{6,2},{3,7},{7,3},{8,12},{12,8},{9,1... | collective-permute-start | bytes 995336 | tf_op jit(solution)/shard_map/ppermute | solution.py:280
  247.0 13.2 %collective-permute-start.61 = (f32[648,128]{1,0:T(8,128)S(1)}, f32[648,128]{1,0:T(8,128)S(1)}, u32[]{:S(2)}, u32[]{:S(2)}) collective-permute-start(f32[648,128]{1,0:T(8,128)S(1)} %add.201), channel_id=1, source_target_pairs={{8,16},{16,8},{9,17},{17,9},{10,18},{18,10},{11,19},{19,11},{12,20... | collective-permute-start | bytes 995336 | tf_op jit(solution)/shard_map/ppermute | solution.py:294
  248.0 12.5 %collective-permute-start.60 = (f32[648,128]{1,0:T(8,128)S(1)}, f32[648,128]{1,0:T(8,128)S(1)}, u32[]{:S(2)}, u32[]{:S(2)}) collective-permute-start(f32[648,128]{1,0:T(8,128)S(1)} %add_add_fusion), channel_id=1, source_target_pairs={{0,8},{8,0},{16,24},{24,16},{1,9},{9,1},{17,25},{25,17},{2,10},{10... | collective-permute-start | bytes 995336 | tf_op jit(solution)/shard_map/ppermute | solution.py:280
  260.9 10.8 %collective-permute-start.63 = (f32[648,128]{1,0:T(8,128)S(1)}, f32[648,128]{1,0:T(8,128)S(1)}, u32[]{:S(2)}, u32[]{:S(2)}) collective-permute-start(f32[648,128]{1,0:T(8,128)S(1)} %get-tuple-element.376.refs_0_.refs_1_), channel_id=1, source_target_pairs={{0,8},{8,0},{16,24},{24,16},{1,9},{9,1},{17,25},{25,17},{2,10},{10... | collective-permute-start | bytes 995336 | tf_op jit(solution)/shard_map/ppermute | solution.py:280
  262.7 9.0 %collective-permute-start.64 = (f32[648,128]{1,0:T(8,128)S(1)}, f32[648,128]{1,0:T(8,128)S(1)}, u32[]{:S(2)}, u32[]{:S(2)}) collective-permute-start(f32[648,128]{1,0:T(8,128)S(1)} %get-tuple-element.376.refs_0_.refs_1_), channel_id=1, source_target_pairs={{8,16},{16,8},{9,17},{17,9},{10,18},{18,10},{11,19},{19,11},{12,20... | collective-permute-start | bytes 995336 | tf_op jit(solution)/shard_map/ppermute | solution.py:294
  263.4 10.8 %collective-permute-start.65 = (f32[648,128]{1,0:T(8,128)S(1)}, f32[648,128]{1,0:T(8,128)S(1)}, u32[]{:S(2)}, u32[]{:S(2)}) collective-permute-start(f32[648,128]{1,0:T(8,128)S(1)} %get-tuple-element.378), channel_id=1, source_target_pairs={{0,4},{4,0},{1,5},{5,1},{2,6},{6,2},{3,7},{7,3},{8,12},{12,8},{9,1... | collective-permute-start | bytes 995336 | tf_op jit(solution)/shard_map/ppermute | solution.py:280
  264.7 12.5 %collective-permute-start.66 = (f32[648,128]{1,0:T(8,128)S(1)}, f32[648,128]{1,0:T(8,128)S(1)}, u32[]{:S(2)}, u32[]{:S(2)}) collective-permute-start(f32[648,128]{1,0:T(8,128)S(1)} %get-tuple-element.379), channel_id=1, source_target_pairs={{0,8},{8,0},{16,24},{24,16},{1,9},{9,1},{17,25},{25,17},{2,10},{10... | collective-permute-start | bytes 995336 | tf_op jit(solution)/shard_map/ppermute | solution.py:280
  266.8 14.0 %collective-permute-start.69 = (f32[648,128]{1,0:T(8,128)S(1)}, f32[648,128]{1,0:T(8,128)S(1)}, u32[]{:S(2)}, u32[]{:S(2)}) collective-permute-start(f32[648,128]{1,0:T(8,128)S(1)} %get-tuple-element.376.refs_0_.refs_1_), channel_id=1, source_target_pairs={{0,4},{4,0},{1,5},{5,1},{2,6},{6,2},{3,7},{7,3},{8,12},{12,8},{9,1... | collective-permute-start | bytes 995336 | tf_op jit(solution)/shard_map/ppermute | solution.py:280
  287.9 10.3 %collective-permute-start.72 = (f32[648,128]{1,0:T(8,128)S(1)}, f32[648,128]{1,0:T(8,128)S(1)}, u32[]{:S(2)}, u32[]{:S(2)}) collective-permute-start(f32[648,128]{1,0:T(8,128)S(1)} %get-tuple-element.442), channel_id=1, source_target_pairs={{0,8},{8,0},{16,24},{24,16},{1,9},{9,1},{17,25},{25,17},{2,10},{10... | collective-permute-start | bytes 995336 | tf_op jit(solution)/shard_map/ppermute | solution.py:280
  301.1 8.9 %collective-permute-start.77 = (f32[648,128]{1,0:T(8,128)S(1)}, f32[648,128]{1,0:T(8,128)S(1)}, u32[]{:S(2)}, u32[]{:S(2)}) collective-permute-start(f32[648,128]{1,0:T(8,128)S(1)} %add.206), channel_id=1, source_target_pairs={{0,8},{8,0},{16,24},{24,16},{1,9},{9,1},{17,25},{25,17},{2,10},{10... | collective-permute-start | bytes 995336 | tf_op jit(solution)/shard_map/ppermute | solution.py:280
  303.0 8.7 %collective-permute-start.74 = (f32[648,128]{1,0:T(8,128)S(1)}, f32[648,128]{1,0:T(8,128)S(1)}, u32[]{:S(2)}, u32[]{:S(2)}) collective-permute-start(f32[648,128]{1,0:T(8,128)S(1)} %broadcast_select_fusion.2.refs_3_), channel_id=1, source_target_pairs={{0,4},{4,0},{1,5},{5,1},{2,6},{6,2},{3,7},{7,3},{8,12},{12,8},{9,1... | collective-permute-start | bytes 995336 | tf_op jit(solution)/shard_map/ppermute | solution.py:280
  304.3 10.7 %collective-permute-start.75 = (f32[648,128]{1,0:T(8,128)S(1)}, f32[648,128]{1,0:T(8,128)S(1)}, u32[]{:S(2)}, u32[]{:S(2)}) collective-permute-start(f32[648,128]{1,0:T(8,128)S(1)} %collective-permute-done.69.refs_4_), channel_id=1, source_target_pairs={{0,8},{8,0},{16,24},{24,16},{1,9},{9,1},{17,25},{25,17},{2,10},{10... | collective-permute-start | bytes 995336 | tf_op jit(solution)/shard_map/ppermute | solution.py:280
  304.6 10.6 %collective-permute-start.76 = (f32[648,128]{1,0:T(8,128)S(1)}, f32[648,128]{1,0:T(8,128)S(1)}, u32[]{:S(2)}, u32[]{:S(2)}) collective-permute-start(f32[648,128]{1,0:T(8,128)S(1)} %add.205), channel_id=1, source_target_pairs={{0,4},{4,0},{1,5},{5,1},{2,6},{6,2},{3,7},{7,3},{8,12},{12,8},{9,1... | collective-permute-start | bytes 995336 | tf_op jit(solution)/shard_map/ppermute | solution.py:280
  315.6 10.7 %collective-permute-start.79 = (f32[648,128]{1,0:T(8,128)S(1)}, f32[648,128]{1,0:T(8,128)S(1)}, u32[]{:S(2)}, u32[]{:S(2)}) collective-permute-start(f32[648,128]{1,0:T(8,128)S(1)} %get-tuple-element.416.refs_0_.refs_7_), channel_id=1, source_target_pairs={{0,8},{8,0},{16,24},{24,16},{1,9},{9,1},{17,25},{25,17},{2,10},{10... | collective-permute-start | bytes 995336 | tf_op jit(solution)/shard_map/ppermute | solution.py:280
  326.4 10.2 %collective-permute-start.85 = (f32[648,128]{1,0:T(8,128)S(1)}, f32[648,128]{1,0:T(8,128)S(1)}, u32[]{:S(2)}, u32[]{:S(2)}) collective-permute-start(f32[648,128]{1,0:T(8,128)S(1)} %get-tuple-element.416.refs_0_.refs_7_), channel_id=1, source_target_pairs={{0,4},{4,0},{1,5},{5,1},{2,6},{6,2},{3,7},{7,3},{8,12},{12,8},{9,1... | collective-permute-start | bytes 995336 | tf_op jit(solution)/shard_map/ppermute | solution.py:280
  327.8 10.7 %collective-permute-start.83 = (f32[648,128]{1,0:T(8,128)S(1)}, f32[648,128]{1,0:T(8,128)S(1)}, u32[]{:S(2)}, u32[]{:S(2)}) collective-permute-start(f32[648,128]{1,0:T(8,128)S(1)} %collective-permute-done.80), channel_id=1, source_target_pairs={{0,8},{8,0},{16,24},{24,16},{1,9},{9,1},{17,25},{25,17},{2,10},{10... | collective-permute-start | bytes 995336 | tf_op jit(solution)/shard_map/ppermute | solution.py:280
  331.4 9.7 %collective-permute-start.82 = (f32[648,128]{1,0:T(8,128)S(1)}, f32[648,128]{1,0:T(8,128)S(1)}, u32[]{:S(2)}, u32[]{:S(2)}) collective-permute-start(f32[648,128]{1,0:T(8,128)S(1)} %fusion.2), channel_id=1, source_target_pairs={{0,2},{2,0},{1,3},{3,1},{4,6},{6,4},{5,7},{7,5},{8,10},{10,8},{9,1... | collective-permute-start | bytes 995336 | tf_op jit(solution)/shard_map/ppermute | solution.py:280
  341.1 8.8 %collective-permute-start.86 = (f32[648,128]{1,0:T(8,128)S(1)}, f32[648,128]{1,0:T(8,128)S(1)}, u32[]{:S(2)}, u32[]{:S(2)}) collective-permute-start(f32[648,128]{1,0:T(8,128)S(1)} %broadcast_select_fusion.1.refs_2_), channel_id=1, source_target_pairs={{0,4},{4,0},{1,5},{5,1},{2,6},{6,2},{3,7},{7,3},{8,12},{12,8},{9,1... | collective-permute-start | bytes 995336 | tf_op jit(solution)/shard_map/ppermute | solution.py:280
  368.9 9.9 %collective-permute-start.91 = (f32[648,128]{1,0:T(8,128)S(1)}, f32[648,128]{1,0:T(8,128)S(1)}, u32[]{:S(2)}, u32[]{:S(2)}) collective-permute-start(f32[648,128]{1,0:T(8,128)S(1)} %fusion.1), channel_id=1, source_target_pairs={{0,2},{2,0},{1,3},{3,1},{4,6},{6,4},{5,7},{7,5},{8,10},{10,8},{9,1... | collective-permute-start | bytes 995336 | tf_op jit(solution)/shard_map/ppermute | solution.py:280
  (35 other events, 208.6 us)
